TPU v7x, 32 devices: a whole 2x2x4 slice. The times are simulated.
32 devices in a mesh: ctx: 4 (over y, x), exp: 8 (over z, core).
Axes of the slice: x: 2, y: 2, z: 4, core: 2. Of those that a mesh axis runs over, the one named last changes fastest.
Arguments:
- queries: bfloat16 [8, 512, 2048], P('exp', 'ctx')
- key_rows: bfloat16 [8, 512, 2048], P('exp', 'ctx')
- value_rows: bfloat16 [8, 512, 2048], P('exp', 'ctx'), may hold values from -6 to 6
- out_grad: bfloat16 [8, 512, 2048], P('exp', 'ctx'), may hold values from -6 to 6
- moe_input: bfloat16 [8, 512, 2048], P('exp', 'ctx'), may hold values from -6 to 6
- routes: int32 [8, 512, 4], P('exp', 'ctx'), may hold values from 0 to 31, all different within a row; in each aligned block of 128 rows (0 to 127, 128 to 255, ..., all dimensions but the last counted through in order) at most 24 rows name the same one
- route_gates: float32 [8, 512, 4], P('exp', 'ctx'), may hold values from 0.1 to 1
- up_weight: bfloat16 [32, 2048, 768], P('exp'), may hold values from -0.125 to 0.125
- down_weight: bfloat16 [32, 768, 2048], P('exp'), may hold values from -0.21875 to 0.21875
Outputs:
- query_grad: bfloat16 [8, 512, 2048], P('exp', 'ctx')
- key_grad: bfloat16 [8, 512, 2048], P('exp', 'ctx')
- value_grad: bfloat16 [8, 512, 2048], P('exp', 'ctx')
- input_grad: bfloat16 [8, 512, 2048], P('exp', 'ctx')
Inputs may be any that keep to these rules, and one draw needn't show every extreme that they name: In the bins of one device no expert is named by more than 24 routes, a bound that some block reaches; the 4 experts of a bin differ.
All inputs are finite; a program needn't handle non-finite values.
Results may differ from a plain program's by a relative error of at most 0.0064.
Values may be sent and summed in bfloat16 or wider, within the bound.
No kernel may reach another device: no remote copies, remote signals or barrier semaphores. Data moves between devices by JAX's collectives and lax.ppermute only.
A program may use at most 128 MiB of HBM per device.

v0:
```python
import jax
import jax.numpy as jnp
from jax import lax
from jax.sharding import PartitionSpec as P

HD = 128
CAP = 24


def silu_slope(preact):
    sigmoid = jax.nn.sigmoid(preact)
    return sigmoid * (1.0 + preact * (1.0 - sigmoid))


def heads_back(query_heads, key_heads, value_heads, grad_heads):
    seq_len = query_heads.shape[0]
    head_count = query_heads.shape[1] // HD
    query_three = query_heads.reshape(seq_len, head_count, HD)
    key_three = key_heads.reshape(seq_len, head_count, HD)
    value_three = value_heads.reshape(seq_len, head_count, HD)
    grad_three = grad_heads.reshape(seq_len, head_count, HD)
    block_rows = 512
    score_scale = HD ** (-0.5)

    def one_block(carried, block_index):
        key_acc, value_acc = carried
        first_row = block_index * block_rows
        query_block = lax.dynamic_slice_in_dim(query_three, first_row, block_rows, 0)
        grad_block = lax.dynamic_slice_in_dim(grad_three, first_row, block_rows, 0)
        scores = (
            jnp.einsum("qhd,khd->hqk", query_block, key_three, preferred_element_type=jnp.float32)
            * score_scale
        )
        probs = jax.nn.softmax(scores, axis=-1)
        prob_grad = jnp.einsum(
            "qhd,khd->hqk", grad_block, value_three, preferred_element_type=jnp.float32
        )
        row_delta = jnp.sum(probs * prob_grad, axis=-1, keepdims=True)
        score_grad = (probs * (prob_grad - row_delta)).astype(jnp.bfloat16)
        rounded = probs.astype(jnp.bfloat16)
        query_part = (
            jnp.einsum("hqk,khd->qhd", score_grad, key_three, preferred_element_type=jnp.float32)
            * score_scale
        ).astype(jnp.bfloat16)
        key_acc = (
            key_acc
            + jnp.einsum(
                "hqk,qhd->khd", score_grad, query_block, preferred_element_type=jnp.float32
            )
            * score_scale
        )
        value_acc = value_acc + jnp.einsum(
            "hqk,qhd->khd", rounded, grad_block, preferred_element_type=jnp.float32
        )
        return ((key_acc, value_acc), query_part)

    zero_acc = jnp.zeros((seq_len, head_count, HD), jnp.float32)
    block_ids = jnp.arange(seq_len // block_rows, dtype=jnp.int32)
    (key_acc, value_acc), query_parts = lax.scan(one_block, (zero_acc, zero_acc), block_ids)
    feature_width = head_count * HD
    query_out = query_parts.reshape(seq_len, feature_width)
    key_out = key_acc.reshape(seq_len, feature_width).astype(jnp.bfloat16)
    value_out = value_acc.reshape(seq_len, feature_width).astype(jnp.bfloat16)
    return (query_out, key_out, value_out)


def attention_back(queries, key_rows, value_rows, out_grad):
    groups = lax.axis_size("ctx")
    bin_count = queries.shape[1]
    model_width = queries.shape[2]
    head_width = model_width // groups
    seq_len = bin_count * groups

    def split_heads(member):
        return member.reshape(1, bin_count, groups, head_width)

    arrived = (
        lax.all_to_all(split_heads(queries), "ctx", split_axis=2, concat_axis=1, tiled=True),
        lax.all_to_all(split_heads(key_rows), "ctx", split_axis=2, concat_axis=1, tiled=True),
        lax.all_to_all(split_heads(value_rows), "ctx", split_axis=2, concat_axis=1, tiled=True),
        lax.all_to_all(split_heads(out_grad), "ctx", split_axis=2, concat_axis=1, tiled=True),
    )
    query_heads = arrived[0].reshape(seq_len, head_width)
    key_heads = arrived[1].reshape(seq_len, head_width)
    value_heads = arrived[2].reshape(seq_len, head_width)
    grad_heads = arrived[3].reshape(seq_len, head_width)
    query_out, key_out, value_out = heads_back(query_heads, key_heads, value_heads, grad_heads)

    def join_heads(member):
        return member.reshape(1, seq_len, 1, head_width)

    departed = (
        lax.all_to_all(join_heads(query_out), "ctx", split_axis=1, concat_axis=2, tiled=True),
        lax.all_to_all(join_heads(key_out), "ctx", split_axis=1, concat_axis=2, tiled=True),
        lax.all_to_all(join_heads(value_out), "ctx", split_axis=1, concat_axis=2, tiled=True),
    )
    return tuple((member.reshape(1, bin_count, model_width) for member in departed))


def expert_tail(gated_recv, slopes, up_weight, down_weight):
    back_grad = jnp.einsum(
        "sjkd,jfd->sjkf", gated_recv, down_weight, preferred_element_type=jnp.float32
    )
    hidden_grad = (back_grad * slopes).astype(jnp.bfloat16)
    return jnp.einsum(
        "sjkf,jdf->sjkd", hidden_grad, up_weight, preferred_element_type=jnp.float32
    ).astype(jnp.bfloat16)


def expert_back(token_recv, gated_recv, up_weight, down_weight):
    preact = jnp.einsum("sjkd,jdf->sjkf", token_recv, up_weight, preferred_element_type=jnp.float32)
    return expert_tail(gated_recv, silu_slope(preact), up_weight, down_weight)


def mixture_back(moe_input, out_grad, routes, route_gates, up_weight, down_weight):
    groups = lax.axis_size("exp")
    bin_count = moe_input.shape[1]
    model_width = moe_input.shape[2]
    top_count = routes.shape[2]
    local_experts = up_weight.shape[0]
    expert_total = local_experts * groups
    route_count = bin_count * top_count
    capacity = CAP
    flat_routes = routes.reshape(route_count)
    onehot = (flat_routes[:, None] == jnp.arange(expert_total, dtype=jnp.int32)[None, :]).astype(
        jnp.int32
    )
    position = jnp.sum((jnp.cumsum(onehot, axis=0) - onehot) * onehot, axis=1)
    slot_index = flat_routes * capacity + position
    source = (
        jnp.full((expert_total * capacity,), route_count, jnp.int32)
        .at[slot_index]
        .set(jnp.arange(route_count, dtype=jnp.int32))
    )
    token_index = source // top_count
    zero_row = jnp.zeros((1, model_width), jnp.bfloat16)
    token_gather = jnp.concatenate([moe_input[0], zero_row], axis=0)[token_index]
    grad_gather = jnp.concatenate([out_grad[0], zero_row], axis=0)[token_index]
    slot_gates = jnp.concatenate([route_gates.reshape(route_count), jnp.zeros((1,), jnp.float32)])[
        source
    ]
    gated_gather = (slot_gates[:, None] * grad_gather.astype(jnp.float32)).astype(jnp.bfloat16)
    layout = (groups, local_experts, capacity, model_width)
    token_send = token_gather.reshape(layout)
    gated_send = gated_gather.reshape(layout)
    result = expert_back(
        lax.all_to_all(token_send, "exp", split_axis=0, concat_axis=0, tiled=True),
        lax.all_to_all(gated_send, "exp", split_axis=0, concat_axis=0, tiled=True),
        up_weight,
        down_weight,
    )
    returned_rows = lax.all_to_all(result, "exp", split_axis=0, concat_axis=0, tiled=True)
    per_route = returned_rows.reshape(expert_total * capacity, model_width)[slot_index]
    summed = jnp.sum(
        per_route.reshape(bin_count, top_count, model_width).astype(jnp.float32), axis=1
    )
    return summed.astype(jnp.bfloat16).reshape(1, bin_count, model_width)


def per_device(
    queries, key_rows, value_rows, out_grad, moe_input, routes, route_gates, up_weight, down_weight
):
    query_grad, key_grad, value_grad = attention_back(queries, key_rows, value_rows, out_grad)
    input_grad = mixture_back(moe_input, out_grad, routes, route_gates, up_weight, down_weight)
    return (query_grad, key_grad, value_grad, input_grad)


def solution(mesh):
    in_specs = (
        P("exp", "ctx", None),
        P("exp", "ctx", None),
        P("exp", "ctx", None),
        P("exp", "ctx", None),
        P("exp", "ctx", None),
        P("exp", "ctx", None),
        P("exp", "ctx", None),
        P("exp", None, None),
        P("exp", None, None),
    )
    out_specs = (
        P("exp", "ctx", None),
        P("exp", "ctx", None),
        P("exp", "ctx", None),
        P("exp", "ctx", None),
    )
    return jax.shard_map(
        per_device, mesh=mesh, in_specs=in_specs, out_specs=out_specs, check_vma=False
    )
```

profile of v0, /device:TPU:0, one launch (start us, length us, event | category | flops | bytes accessed | tf_op | source)
XLA Modules:
  0.0 363.6 jit_solution(3389192147562811736)
XLA Ops:
  3.1 5.3 %all-to-all-start.1 = ((bf16[1,128,4,512]{3,1,0,2:T(8,128)(2,1)}), bf16[1,128,4,512]{3,1,0,2:T(8,128)(2,1)S(1)}, u32[]{:S(2)}, u32[]{:S(2)}) async-start(bf16[1,128,4,512]{3,1,0,2:T(8,128)(2,1)} %copy.138), calls=%async_computation.1 | async-start | bytes 1048576 | tf_op jit(solution)/shard_map/all_to_all | solution.py:79
  9.7 6.7 %all-to-all-done.1 = bf16[1,128,4,512]{3,1,0,2:T(8,128)(2,1)S(1)} async-done(((bf16[1,128,4,512]{3,1,0,2:T(8,128)(2,1)}), bf16[1,128,4,512]{3,1,0,2:T(8,128)(2,1)S(1)}, u32[]{:S(2)}, u32[]{:S(2)}) %all-to-all-start.1) | async-done | bytes 524320 | tf_op jit(solution)/shard_map/all_to_all | solution.py:79
  16.4 3.5 all-to-all-start
  23.0 3.9 %all-to-all-done = bf16[1,128,4,512]{3,1,0,2:T(8,128)(2,1)S(1)} async-done(((bf16[1,128,4,512]{3,1,0,2:T(8,128)(2,1)}), bf16[1,128,4,512]{3,1,0,2:T(8,128)(2,1)S(1)}, u32[]{:S(2)}, u32[]{:S(2)}) %all-to-all-start) | async-done | bytes 524320 | tf_op jit(solution)/shard_map/all_to_all | solution.py:78
  27.0 3.5 all-to-all-start.2
  32.0 5.0 %all-to-all-done.2 = bf16[1,128,4,512]{3,1,0,2:T(8,128)(2,1)S(1)} async-done(((bf16[1,128,4,512]{3,1,0,2:T(8,128)(2,1)}), bf16[1,128,4,512]{3,1,0,2:T(8,128)(2,1)S(1)}, u32[]{:S(2)}, u32[]{:S(2)}) %all-to-all-start.2) | async-done | bytes 524320 | tf_op jit(solution)/shard_map/all_to_all | solution.py:81
  37.0 3.5 all-to-all-start.3
  40.7 3.0 scatter_custom_fusion
  47.2 3.4 fusion.57
  50.6 3.0 multiply_reduce_fusion
  56.5 2.4 copy.149
  59.4 4.5 %reduce.3 = bf16[512,512]{1,0:T(8,128)(2,1)} reduce(bf16[512,1,1,512]{3,2,1,0:T(2,128)(2,1)S(1)} %bitcast.150, bf16[]{:T(256)} %broadcast.124), dimensions={1,2}, to_apply=%bitcast.127.reduce_sub_computation | reduce | bytes 1048578
  64.0 2.3 reshape.199
  66.2 4.3 %all-to-all-start.4 = ((bf16[4,2,32768]{2,1,0:T(2,128)(2,1)}), bf16[4,2,32768]{2,1,0:T(2,128)(2,1)}, u32[]{:S(2)}, u32[]{:S(2)}) async-start(bf16[4,2,32768]{2,1,0:T(2,128)(2,1)} %reshape.199), calls=%async_computation.4 | async-start | bytes 1048576 | tf_op jit(solution)/shard_map/all_to_all | solution.py:93
  70.6 3.2 gather_fusion
  73.9 4.3 %gather_fusion.1 = bf16[768,2048]{1,0:T(8,128)(2,1)} fusion(bf16[129,2048]{1,0:T(8,128)(2,1)S(1)} %concatenate.10, s32[1024]{0:T(1024)S(1)} %get-tuple-element.42), kind=kCustom, calls=%fused_computation.1 | custom fusion | bytes 6294528 | tf_op jit(solution)/shard_map/gather | solution.py:138
  79.8 3.7 %copy.153 = bf16[1,512,1,512]{3,2,0,1:T(2,128)(2,1)} copy(bf16[1,512,1,512]{1,3,2,0:T(8,128)(2,1)} %bitcast.170) | data formatting | bytes 1048576 | tf_op jit(solution)/shard_map/convert_element_type | solution.py:62
  83.6 5.5 %reduce.4 = bf16[512,512]{1,0:T(8,128)(2,1)} reduce(bf16[512,1,1,512]{3,2,1,0:T(2,128)(2,1)} %bitcast.152, bf16[]{:T(256)} %broadcast.124), dimensions={1,2}, to_apply=%bitcast.129.reduce_sub_computation | reduce | bytes 1048578
  89.1 2.2 reshape.201
  91.3 4.2 %all-to-all-start.5 = ((bf16[4,2,32768]{2,1,0:T(2,128)(2,1)}), bf16[4,2,32768]{2,1,0:T(2,128)(2,1)}, u32[]{:S(2)}, u32[]{:S(2)}) async-start(bf16[4,2,32768]{2,1,0:T(2,128)(2,1)} %reshape.201), calls=%async_computation.5 | async-start | bytes 1048576 | tf_op jit(solution)/shard_map/all_to_all | solution.py:94
  95.5 2.3 fusion.7
  97.7 4.4 %all-to-all-done.5 = bf16[4,2,32768]{2,1,0:T(2,128)(2,1)} async-done(((bf16[4,2,32768]{2,1,0:T(2,128)(2,1)}), bf16[4,2,32768]{2,1,0:T(2,128)(2,1)}, u32[]{:S(2)}, u32[]{:S(2)}) %all-to-all-start.5) | async-done | bytes 524320 | tf_op jit(solution)/shard_map/all_to_all | solution.py:94
  102.1 4.9 %all-to-all-start.7 = ((bf16[8,4,24,2048]{3,2,1,0:T(8,128)(2,1)}), bf16[8,4,24,2048]{3,2,1,0:T(8,128)(2,1)}, u32[]{:S(2)}, u32[]{:S(2)}) async-start(bf16[8,4,24,2048]{3,2,1,0:T(8,128)(2,1)} %fusion.7), calls=%async_computation.7 | async-start | bytes 6291456 | tf_op jit(solution)/shard_map/all_to_all | solution.py:148
  107.1 4.3 %gather_fusion.2 = bf16[768,2048]{1,0:T(8,128)(2,1)} fusion(bf16[129,2048]{1,0:T(8,128)(2,1)S(1)} %concatenate.11, s32[1024]{0:T(1024)S(1)} %get-tuple-element.42), kind=kCustom, calls=%fused_computation.2 | custom fusion | bytes 6294528 | tf_op jit(solution)/shard_map/gather | solution.py:137
  111.4 67.3 %all-to-all-done.7 = bf16[8,4,24,2048]{3,2,1,0:T(8,128)(2,1)} async-done(((bf16[8,4,24,2048]{3,2,1,0:T(8,128)(2,1)}), bf16[8,4,24,2048]{3,2,1,0:T(8,128)(2,1)}, u32[]{:S(2)}, u32[]{:S(2)}) %all-to-all-start.7) | async-done | bytes 3145760 | tf_op jit(solution)/shard_map/all_to_all | solution.py:148
  178.7 4.8 %all-to-all-start.8 = ((bf16[8,4,24,2048]{3,2,1,0:T(8,128)(2,1)}), bf16[8,4,24,2048]{3,2,1,0:T(8,128)(2,1)}, u32[]{:S(2)}, u32[]{:S(2)}) async-start(bf16[8,4,24,2048]{3,2,1,0:T(8,128)(2,1)} %bitcast.145), calls=%async_computation.8 | async-start | bytes 6291456 | tf_op jit(solution)/shard_map/all_to_all | solution.py:147
  183.5 3.0 fusion.37
  187.4 3.7 %reduce.5 = bf16[512,512]{1,0:T(8,128)(2,1)S(1)} reduce(bf16[512,1,1,512]{3,2,1,0:T(2,128)(2,1)S(1)} %bitcast.151, bf16[]{:T(256)} %broadcast.124), dimensions={1,2}, to_apply=%bitcast.131.reduce_sub_computation | reduce | bytes 1048578
  192.3 11.2 %fusion.5 = f32[4,8,24,768]{3,2,1,0:T(8,128)} fusion(bf16[4,768,2048]{2,1,0:T(8,128)(2,1)} %param.17, bf16[8,4,24,2048]{3,2,1,0:T(8,128)(2,1)} %all-to-all-done.7), kind=kOutput, calls=%fused_computation.10 | convolution fusion | flops 2415919104 | bytes 18087936 | tf_op jit(solution)/shard_map/sjkd,jfd->sjkf/dot_general | solution.py:101
  203.5 51.5 %all-to-all-done.8 = bf16[8,4,24,2048]{3,2,1,0:T(8,128)(2,1)} async-done(((bf16[8,4,24,2048]{3,2,1,0:T(8,128)(2,1)}), bf16[8,4,24,2048]{3,2,1,0:T(8,128)(2,1)}, u32[]{:S(2)}, u32[]{:S(2)}) %all-to-all-start.8) | async-done | bytes 3145760 | tf_op jit(solution)/shard_map/all_to_all | solution.py:147
  255.0 4.1 %all-to-all-start.6 = ((bf16[4,2,32768]{2,1,0:T(2,128)(2,1)}), bf16[4,2,32768]{2,1,0:T(2,128)(2,1)}, u32[]{:S(2)}, u32[]{:S(2)}) async-start(bf16[4,2,32768]{2,1,0:T(2,128)(2,1)} %reshape.203), calls=%async_computation.6 | async-start | bytes 1048576 | tf_op jit(solution)/shard_map/all_to_all | solution.py:95
  259.1 17.0 %fusion.16 = bf16[8,4,24,2048]{3,2,0,1:T(8,128)(2,1)S(1)} fusion(bf16[4,2048,768]{2,1,0:T(8,128)(2,1)} %param.16, f32[4,8,24,768]{3,2,1,0:T(8,128)} %fusion.5, bf16[8,4,24,2048]{3,2,1,0:T(8,128)(2,1)} %all-to-all-done.8), kind=kOutput, calls=%fused_computation.22 | convolution fusion | flops 4838719488 | bytes 21233664 | tf_op jit(solution)/shard_map/sjkf,jdf->sjkd/dot_general | solution.py:105
  278.0 3.9 %all-to-all-start.9 = ((bf16[8,4,24,2048]{3,2,1,0:T(8,128)(2,1)}), bf16[8,4,24,2048]{3,2,1,0:T(8,128)(2,1)S(1)}, u32[]{:S(2)}, u32[]{:S(2)}) async-start(bf16[8,4,24,2048]{3,2,1,0:T(8,128)(2,1)} %copy.166), calls=%async_computation.9 | async-start | bytes 6291456 | tf_op jit(solution)/shard_map/all_to_all | solution.py:152
  282.0 3.5 reshape.200
  285.4 2.1 copy.175
  287.6 2.0 copy.150
  289.6 2.0 copy.167
  291.7 3.5 reshape.202
  295.1 2.1 copy.176
  297.3 2.0 copy.154
  299.3 2.0 copy.168
  301.3 3.5 reshape.204
  304.8 2.1 copy.177
  309.0 2.0 copy.169
  311.0 42.4 %all-to-all-done.9 = bf16[8,4,24,2048]{3,2,1,0:T(8,128)(2,1)S(1)} async-done(((bf16[8,4,24,2048]{3,2,1,0:T(8,128)(2,1)}), bf16[8,4,24,2048]{3,2,1,0:T(8,128)(2,1)S(1)}, u32[]{:S(2)}, u32[]{:S(2)}) %all-to-all-start.9) | async-done | bytes 3145760 | tf_op jit(solution)/shard_map/all_to_all | solution.py:152
  353.4 3.3 gather_fusion.3
  356.7 2.7 reshape.148
  359.5 3.9 %reduce_sum.47 = bf16[128,2048]{1,0:T(8,128)(2,1)} reduce(bf16[128,4,2048]{2,1,0:T(4,128)(2,1)S(1)} %reshape.148, bf16[]{:T(256)} %constant.58.clone.1), dimensions={1}, to_apply=%region_7.8 | reduce | flops 786432 | bytes 2621442 | tf_op jit(solution)/shard_map/reduce_sum | solution.py:154
  (75 shorter events, 23.1 us)
Async XLA Ops:
  0.6 7.7 %copy-start.4 = (bf16[1,128,2048]{2,1,0:T(8,128)(2,1)S(1)}, bf16[1,128,2048]{2,1,0:T(8,128)(2,1)}, u32[]{:S(2)}) copy-start(bf16[1,128,2048]{2,1,0:T(8,128)(2,1)} %param.9) | copy-start | bytes 1572868
  0.6 19.2 %copy-start.11 = (s32[1,128,4]{1,2,0:T(4,128)S(1)}, s32[1,128,4]{1,2,0:T(4,128)}, u32[]{:S(2)}) copy-start(s32[1,128,4]{1,2,0:T(4,128)} %param.14) | copy-start | bytes 6148
  0.7 19.6 %copy-start.2 = (bf16[1,128,2048]{2,1,0:T(8,128)(2,1)S(1)}, bf16[1,128,2048]{2,1,0:T(8,128)(2,1)}, u32[]{:S(2)}) copy-start(bf16[1,128,2048]{2,1,0:T(8,128)(2,1)} %param.12) | copy-start | bytes 1572868
  3.1 18.4 %copy-start.5 = (bf16[1,128,2048]{2,1,0:T(8,128)(2,1)S(1)}, bf16[1,128,2048]{2,1,0:T(8,128)(2,1)}, u32[]{:S(2)}) copy-start(bf16[1,128,2048]{2,1,0:T(8,128)(2,1)} %param.11) | copy-start | bytes 1572868
  3.1 13.3 %all-to-all-start.1 = ((bf16[1,128,4,512]{3,1,0,2:T(8,128)(2,1)}), bf16[1,128,4,512]{3,1,0,2:T(8,128)(2,1)S(1)}, u32[]{:S(2)}, u32[]{:S(2)}) async-start(bf16[1,128,4,512]{3,1,0,2:T(8,128)(2,1)} %copy.138), calls=%async_computation.1 | async-start | bytes 1048576 | tf_op jit(solution)/shard_map/all_to_all | solution.py:79
  16.4 10.6 %all-to-all-start = ((bf16[1,128,4,512]{3,1,0,2:T(8,128)(2,1)}), bf16[1,128,4,512]{3,1,0,2:T(8,128)(2,1)S(1)}, u32[]{:S(2)}, u32[]{:S(2)}) async-start(bf16[1,128,4,512]{3,1,0,2:T(8,128)(2,1)} %copy.136), calls=%async_computation | async-start | bytes 1048576 | tf_op jit(solution)/shard_map/all_to_all | solution.py:78
  20.2 20.3 %copy-start.12 = (f32[1,128,4]{1,2,0:T(4,128)S(1)}, f32[1,128,4]{1,2,0:T(4,128)}, u32[]{:S(2)}) copy-start(f32[1,128,4]{1,2,0:T(4,128)} %param.15) | copy-start | bytes 6148
  27.0 10.0 %all-to-all-start.2 = ((bf16[1,128,4,512]{3,1,0,2:T(8,128)(2,1)}), bf16[1,128,4,512]{3,1,0,2:T(8,128)(2,1)S(1)}, u32[]{:S(2)}, u32[]{:S(2)}) async-start(bf16[1,128,4,512]{3,1,0,2:T(8,128)(2,1)} %copy.142), calls=%async_computation.2 | async-start | bytes 1048576 | tf_op jit(solution)/shard_map/all_to_all | solution.py:81
  37.0 10.0 %all-to-all-start.3 = ((bf16[1,128,4,512]{3,1,0,2:T(8,128)(2,1)}), bf16[1,128,4,512]{3,1,0,2:T(8,128)(2,1)S(1)}, u32[]{:S(2)}, u32[]{:S(2)}) async-start(bf16[1,128,4,512]{3,1,0,2:T(8,128)(2,1)} %copy.144), calls=%async_computation.3 | async-start | bytes 1048576 | tf_op jit(solution)/shard_map/all_to_all | solution.py:80
  44.7 5.9 %copy-start.8 = (bf16[512,4,128]{0,2,1:T(8,128)(2,1)}, bf16[512,4,128]{0,2,1:T(8,128)(2,1)S(1)}, u32[]{:S(2)}) copy-start(bf16[512,4,128]{0,2,1:T(8,128)(2,1)S(1)} %copy.152) | copy-start | bytes 1572868
  45.1 5.5 %copy-start.6 = (bf16[512,4,128]{0,2,1:T(8,128)(2,1)}, bf16[512,4,128]{0,2,1:T(8,128)(2,1)S(1)}, u32[]{:S(2)}) copy-start(bf16[512,4,128]{0,2,1:T(8,128)(2,1)S(1)} %copy.156) | copy-start | bytes 1572868
  50.6 3.5 copy-start.1
  64.0 9.9 %copy-start.3 = (bf16[1,128,2048]{2,1,0:T(8,128)(2,1)S(1)}, bf16[1,128,2048]{2,1,0:T(8,128)(2,1)}, u32[]{:S(2)}) copy-start(bf16[1,128,2048]{2,1,0:T(8,128)(2,1)} %param.12) | copy-start | bytes 1572868
  66.2 25.0 %all-to-all-start.4 = ((bf16[4,2,32768]{2,1,0:T(2,128)(2,1)}), bf16[4,2,32768]{2,1,0:T(2,128)(2,1)}, u32[]{:S(2)}, u32[]{:S(2)}) async-start(bf16[4,2,32768]{2,1,0:T(2,128)(2,1)} %reshape.199), calls=%async_computation.4 | async-start | bytes 1048576 | tf_op jit(solution)/shard_map/all_to_all | solution.py:93
  73.9 4.3 %copy-start.9 = (bf16[512,4,128]{0,2,1:T(8,128)(2,1)S(1)}, bf16[512,4,128]{0,2,1:T(8,128)(2,1)}, u32[]{:S(2)}) copy-start(bf16[512,4,128]{0,2,1:T(8,128)(2,1)} %copy-done.8) | copy-start | bytes 1572868
  79.8 15.6 %copy-start = (bf16[768,2048]{1,0:T(8,128)(2,1)S(1)}, bf16[768,2048]{1,0:T(8,128)(2,1)}, u32[]{:S(2)}) copy-start(bf16[768,2048]{1,0:T(8,128)(2,1)} %gather_fusion.1) | copy-start | bytes 9437188
  91.3 10.9 %all-to-all-start.5 = ((bf16[4,2,32768]{2,1,0:T(2,128)(2,1)}), bf16[4,2,32768]{2,1,0:T(2,128)(2,1)}, u32[]{:S(2)}, u32[]{:S(2)}) async-start(bf16[4,2,32768]{2,1,0:T(2,128)(2,1)} %reshape.201), calls=%async_computation.5 | async-start | bytes 1048576 | tf_op jit(solution)/shard_map/all_to_all | solution.py:94
  97.7 9.3 %copy-start.10 = (bf16[1,128,2048]{2,1,0:T(8,128)(2,1)S(1)}, bf16[1,128,2048]{2,1,0:T(8,128)(2,1)}, u32[]{:S(2)}) copy-start(bf16[1,128,2048]{2,1,0:T(8,128)(2,1)} %param.13) | copy-start | bytes 1572868
  102.1 76.5 %all-to-all-start.7 = ((bf16[8,4,24,2048]{3,2,1,0:T(8,128)(2,1)}), bf16[8,4,24,2048]{3,2,1,0:T(8,128)(2,1)}, u32[]{:S(2)}, u32[]{:S(2)}) async-start(bf16[8,4,24,2048]{3,2,1,0:T(8,128)(2,1)} %fusion.7), calls=%async_computation.7 | async-start | bytes 6291456 | tf_op jit(solution)/shard_map/all_to_all | solution.py:148
  178.7 4.8 %copy-start.7 = (bf16[512,4,128]{0,2,1:T(8,128)(2,1)S(1)}, bf16[512,4,128]{0,2,1:T(8,128)(2,1)}, u32[]{:S(2)}) copy-start(bf16[512,4,128]{0,2,1:T(8,128)(2,1)} %copy-done.6) | copy-start | bytes 1572868
  178.7 76.3 %all-to-all-start.8 = ((bf16[8,4,24,2048]{3,2,1,0:T(8,128)(2,1)}), bf16[8,4,24,2048]{3,2,1,0:T(8,128)(2,1)}, u32[]{:S(2)}, u32[]{:S(2)}) async-start(bf16[8,4,24,2048]{3,2,1,0:T(8,128)(2,1)} %bitcast.145), calls=%async_computation.8 | async-start | bytes 6291456 | tf_op jit(solution)/shard_map/all_to_all | solution.py:147
  255.0 23.0 %all-to-all-start.6 = ((bf16[4,2,32768]{2,1,0:T(2,128)(2,1)}), bf16[4,2,32768]{2,1,0:T(2,128)(2,1)}, u32[]{:S(2)}, u32[]{:S(2)}) async-start(bf16[4,2,32768]{2,1,0:T(2,128)(2,1)} %reshape.203), calls=%async_computation.6 | async-start | bytes 1048576 | tf_op jit(solution)/shard_map/all_to_all | solution.py:95
  278.0 75.4 %all-to-all-start.9 = ((bf16[8,4,24,2048]{3,2,1,0:T(8,128)(2,1)}), bf16[8,4,24,2048]{3,2,1,0:T(8,128)(2,1)S(1)}, u32[]{:S(2)}, u32[]{:S(2)}) async-start(bf16[8,4,24,2048]{3,2,1,0:T(8,128)(2,1)} %copy.166), calls=%async_computation.9 | async-start | bytes 6291456 | tf_op jit(solution)/shard_map/all_to_all | solution.py:152
where the time goes:
time: 369 us; the launch traced here: 364 us
  waiting for transfers between devices  183 us (50%)
  local copies, waits for them, and re-layouts  74.3 us (20%)
  starting transfers between devices  41.9 us (11%)
  matrix products  40.6 us (11%)
  other arithmetic  22.4 us (6%)
    all_to_all x1, waiting for transfers between devices, mixture_back(): lax.all_to_all(gated_send, 'exp', split_axis=0, concat_axis=0, tiled=True)  67.3 us
    all_to_all x1, waiting for transfers between devices, mixture_back(): lax.all_to_all(token_send, 'exp', split_axis=0, concat_axis=0, tiled=True)  51.5 us
    all_to_all x1, waiting for transfers between devices, mixture_back(): lax.all_to_all(result, 'exp', split_axis=0, concat_axis=0, tiled=True)  42.4 us
    unnamed x45, local copies, waits for them, and re-layouts  32 us
    dot_general x1, matrix products, expert_tail(): jnp.einsum('sjkf,jdf->sjkd', hidden_grad, up_weight, preferred_element_ty...  17 us
    unnamed x3, other arithmetic  13.8 us
    dot_general x1, matrix products, expert_tail(): jnp.einsum('sjkd,jfd->sjkf', gated_recv, down_weight, preferred_element_t...  11.2 us
  transfers between devices with their start and end apart: 10, of which 8 were waited for; matrix products, arithmetic and copies ran while one was open for 29% of the time, Pallas kernels for 0%

commit v1 on v0

v1 whole, which is shorter than its diff:
```python
import functools

import jax
import jax.numpy as jnp
from jax import lax
from jax.experimental import pallas as pl
from jax.experimental.pallas import tpu as pltpu
from jax.sharding import PartitionSpec as P

HD = 128
CAP = 24
VMEM_BYTES = 44 * 1024 * 1024
NT = (((1,), (1,)), ((), ()))
TN = (((0,), (0,)), ((), ()))


def dot_nt(left, right):
    return lax.dot_general(left, right, NT, preferred_element_type=jnp.float32)


def dot_tn(left, right):
    return lax.dot_general(left, right, TN, preferred_element_type=jnp.float32)


def dot_nn(left, right):
    return jnp.dot(left, right, preferred_element_type=jnp.float32)


def silu_slope(preact):
    sigmoid = jax.nn.sigmoid(preact)
    return sigmoid * (1.0 + preact * (1.0 - sigmoid))


def pack_kernel(group_ref, *refs):
    members, blocks = refs[:4], refs[4:]
    width = blocks[0].shape[2]
    for place, block in enumerate(blocks):
        first = pl.multiple_of(group_ref[place] * width, 128)
        for row, member in enumerate(members):
            block[row] = member[:, pl.ds(first, width)]


def pack_groups(group_ids, members, groups):
    bins, width = members[0].shape
    block = jax.ShapeDtypeStruct((4, bins, width // groups), jnp.bfloat16)
    return pl.pallas_call(
        pack_kernel,
        out_shape=[block] * groups,
        in_specs=[pl.BlockSpec(memory_space=pltpu.SMEM)]
        + [pl.BlockSpec(memory_space=pltpu.VMEM)] * 4,
        out_specs=[pl.BlockSpec(memory_space=pltpu.VMEM)] * groups,
        compiler_params=pltpu.CompilerParams(vmem_limit_bytes=VMEM_BYTES),
        cost_estimate=pl.CostEstimate(
            flops=0, bytes_accessed=16 * bins * width, transcendentals=0
        ),
        name="pack_groups",
    )(group_ids, *members)


def unpack_kernel(group_ref, *refs):
    blocks, outs = refs[:-3], refs[-3:]
    width = blocks[0].shape[2]
    for place, block in enumerate(blocks):
        first = pl.multiple_of(group_ref[place] * width, 128)
        for row, out in enumerate(outs):
            out[:, pl.ds(first, width)] = block[row]


def unpack_groups(group_ids, blocks):
    groups = len(blocks)
    bins, width = blocks[0].shape[1], blocks[0].shape[2] * groups
    out = jax.ShapeDtypeStruct((bins, width), jnp.bfloat16)
    return pl.pallas_call(
        unpack_kernel,
        out_shape=[out] * 3,
        in_specs=[pl.BlockSpec(memory_space=pltpu.SMEM)]
        + [pl.BlockSpec(memory_space=pltpu.VMEM)] * groups,
        out_specs=[pl.BlockSpec(memory_space=pltpu.VMEM)] * 3,
        compiler_params=pltpu.CompilerParams(vmem_limit_bytes=VMEM_BYTES),
        cost_estimate=pl.CostEstimate(
            flops=0, bytes_accessed=12 * bins * width, transcendentals=0
        ),
        name="unpack_groups",
    )(group_ids, *blocks)


def heads_kernel(*refs):
    count = len(refs) // 2
    blocks, outs = refs[:count], refs[count:]
    bins = blocks[0].shape[1]
    scale = HD ** (-0.5)
    query, key, value, grad = (
        jnp.concatenate([block[row] for block in blocks], axis=0) for row in range(4)
    )
    scores = dot_nt(key, query) * scale
    powers = jnp.exp(scores - jnp.max(scores, axis=0, keepdims=True))
    probs = powers * (1.0 / jnp.sum(powers, axis=0, keepdims=True))
    prob_grad = dot_nt(value, grad)
    row_delta = jnp.sum(probs * prob_grad, axis=0, keepdims=True)
    score_grad = (probs * (prob_grad - row_delta)).astype(jnp.bfloat16)
    results = (
        dot_tn(score_grad, key) * scale,
        dot_nn(score_grad, query) * scale,
        dot_nn(probs.astype(jnp.bfloat16), grad),
    )
    for row, result in enumerate(results):
        result = result.astype(jnp.bfloat16)
        for place, out in enumerate(outs):
            out[row] = result[place * bins : (place + 1) * bins]


def heads_back(blocks):
    groups = len(blocks)
    bins, width = blocks[0].shape[1:]
    rows = bins * groups
    heads = width // HD
    return pl.pallas_call(
        heads_kernel,
        grid=(heads,),
        out_shape=[jax.ShapeDtypeStruct((3, bins, width), jnp.bfloat16)] * groups,
        in_specs=[pl.BlockSpec((4, bins, HD), lambda h: (0, 0, h))] * groups,
        out_specs=[pl.BlockSpec((3, bins, HD), lambda h: (0, 0, h))] * groups,
        compiler_params=pltpu.CompilerParams(vmem_limit_bytes=VMEM_BYTES),
        cost_estimate=pl.CostEstimate(
            flops=20 * heads * rows * rows * HD,
            bytes_accessed=14 * rows * width,
            transcendentals=heads * rows * rows,
        ),
        name="heads_back",
    )(*blocks)


def attention_back(queries, key_rows, value_rows, out_grad):
    groups = lax.axis_size("ctx")
    me = lax.axis_index("ctx")
    group_ids = jnp.stack([me ^ place for place in range(groups)]).astype(jnp.int32)

    def exchange(block, place):
        if place == 0:
            return block
        return lax.ppermute(block, "ctx", [(i, i ^ place) for i in range(groups)])

    blocks = pack_groups(group_ids, (queries, key_rows, value_rows, out_grad), groups)
    blocks = [exchange(block, place) for place, block in enumerate(blocks)]
    results = heads_back(blocks)
    results = [exchange(block, place) for place, block in enumerate(results)]
    return unpack_groups(group_ids, results)


def expert_kernel(sources, top, meta_ref, *refs):
    token_refs, grad_refs = refs[:sources], refs[sources : 2 * sources]
    up_ref, down_ref = refs[2 * sources : 2 * sources + 2]
    out_refs = refs[2 * sources + 2 : 3 * sources + 2]
    pick_ref, token_rows, gated_rows, back_rows = refs[3 * sources + 2 :]
    bins = token_refs[0].shape[0]
    slots = sources * CAP
    experts = pick_ref.shape[0] // slots
    expert = pl.program_id(0)

    @pl.when(expert == 0)
    def _():
        earlier = lax.broadcasted_iota(jnp.int32, (bins, bins), 0)
        later = lax.broadcasted_iota(jnp.int32, (bins, bins), 1)
        before = (earlier < later).astype(jnp.bfloat16)
        slot = lax.broadcasted_iota(jnp.int32, (slots, bins), 0).astype(jnp.float32)
        gates = [jnp.zeros((slots, 1), jnp.float32)] * experts
        for source in range(sources):
            named = meta_ref[source, :top]
            weights = meta_ref[source, top:]
            hits = [(named == float(local)).astype(jnp.float32) for local in range(experts)]
            chosen = [jnp.sum(hit, axis=0, keepdims=True) for hit in hits]
            stacked = jnp.concatenate(chosen, axis=0)
            position = dot_nn(stacked.astype(jnp.bfloat16), before)
            for local in range(experts):
                place = jnp.where(
                    chosen[local] > 0.0, position[local : local + 1] + float(source * CAP), -1.0
                )
                pick = (slot == place).astype(jnp.float32)
                gate = jnp.sum(hits[local] * weights, axis=0, keepdims=True)
                gates[local] = gates[local] + jnp.sum(pick * gate, axis=1, keepdims=True)
                pick_ref[
                    local * slots : (local + 1) * slots, source * bins : (source + 1) * bins
                ] = pick.astype(jnp.bfloat16)
        picks = pick_ref[...]
        tokens = jnp.concatenate([ref[...] for ref in token_refs], axis=0)
        token_rows[...] = dot_nn(picks, tokens).astype(jnp.bfloat16)
        grads = jnp.concatenate([ref[...] for ref in grad_refs], axis=0)
        gate_column = jnp.concatenate(gates, axis=0)
        gated_rows[...] = (gate_column * dot_nn(picks, grads)).astype(jnp.bfloat16)

    rows = pl.ds(pl.multiple_of(expert * slots, 16), slots)
    preact = dot_nn(token_rows[rows, :], up_ref[0])
    back_grad = dot_nt(gated_rows[rows, :], down_ref[0])
    hidden_grad = (back_grad * silu_slope(preact)).astype(jnp.bfloat16)
    back_rows[rows, :] = dot_nt(hidden_grad, up_ref[0]).astype(jnp.bfloat16)

    @pl.when(expert == experts - 1)
    def _():
        sums = dot_tn(pick_ref[...], back_rows[...])
        for source, out in enumerate(out_refs):
            out[...] = sums[source * bins : (source + 1) * bins].astype(out.dtype)


def expert_back(meta, tokens, grads, up_weight, down_weight, top):
    sources = len(tokens)
    bins, width = tokens[0].shape
    experts, _, hidden = up_weight.shape
    slots = sources * CAP
    whole = pl.BlockSpec((bins, width), lambda e: (0, 0))
    return pl.pallas_call(
        functools.partial(expert_kernel, sources, top),
        grid=(experts,),
        out_shape=[
            jax.ShapeDtypeStruct((bins, width), jnp.bfloat16 if source % 2 else jnp.float32)
            for source in range(sources)
        ],
        in_specs=[pl.BlockSpec(meta.shape, lambda e: (0, 0, 0))]
        + [whole] * (2 * sources)
        + [
            pl.BlockSpec((1, width, hidden), lambda e: (e, 0, 0)),
            pl.BlockSpec((1, hidden, width), lambda e: (e, 0, 0)),
        ],
        out_specs=[whole] * sources,
        scratch_shapes=[
            pltpu.VMEM((experts * slots, sources * bins), jnp.bfloat16),
            pltpu.VMEM((experts * slots, width), jnp.bfloat16),
            pltpu.VMEM((experts * slots, width), jnp.bfloat16),
            pltpu.VMEM((experts * slots, width), jnp.bfloat16),
        ],
        compiler_params=pltpu.CompilerParams(vmem_limit_bytes=VMEM_BYTES),
        cost_estimate=pl.CostEstimate(
            flops=6 * experts * slots * width * hidden,
            bytes_accessed=4 * experts * width * hidden + 8 * sources * bins * width,
            transcendentals=experts * slots * hidden,
        ),
        name="expert_back",
    )(meta, *tokens, *grads, up_weight, down_weight)


def mixture_back(moe_input, out_grad, routes, route_gates, up_weight, down_weight):
    members = lax.axis_size("exp")
    me = lax.axis_index("exp")
    chips = members // 2
    top = routes.shape[1]
    first_expert = me * up_weight.shape[0]

    def swap(block):
        return lax.ppermute(block, "exp", [(i, i ^ 1) for i in range(members)])

    def hop(block, step):
        return lax.ppermute(
            block, "exp", [(i, (i + 2 * step) % members) for i in range(members)]
        )

    half = chips // 2
    offsets = [[0]]
    for distance in range(1, half):
        offsets.append([-distance, distance])
    offsets.append([half])

    meta = jnp.concatenate([routes.T.astype(jnp.float32), route_gates.T], axis=0)
    metas = lax.all_gather(meta, "exp")
    metas = metas.at[:, :top].add(-first_expert.astype(jnp.float32))
    order = jnp.stack(
        [
            (me + 2 * offset) % members ^ core
            for group in offsets
            for offset in group
            for core in range(2)
        ]
    )
    metas = metas[order]

    tokens, grads = {0: moe_input}, {0: out_grad}
    for distance in range(1, half):
        for sign in (1, -1):
            offset = -sign * distance
            tokens[offset] = hop(tokens[offset + sign], sign)
            grads[offset] = hop(grads[offset + sign], sign)
    tokens[half] = hop(tokens[1 - half], 1)
    grads[half] = hop(grads[half - 1], -1)

    total = None
    done = 0
    arrived = []
    for group in offsets:
        group_tokens, group_grads = [], []
        for offset in group:
            group_tokens += [tokens[offset], swap(tokens[offset])]
            group_grads += [grads[offset], swap(grads[offset])]
        count = len(group_tokens)
        sums = expert_back(
            metas[done : done + count], group_tokens, group_grads, up_weight, down_weight, top
        )
        done += count
        for place, offset in enumerate(group):
            both = sums[2 * place] + swap(sums[2 * place + 1]).astype(jnp.float32)
            if offset == 0:
                total = both
            else:
                arrived.append(hop(both.astype(jnp.bfloat16), offset))
    for part in arrived:
        total = total + part.astype(jnp.float32)
    return total.astype(jnp.bfloat16)


def per_device(
    queries, key_rows, value_rows, out_grad, moe_input, routes, route_gates, up_weight, down_weight
):
    query_grad, key_grad, value_grad = attention_back(
        queries[0], key_rows[0], value_rows[0], out_grad[0]
    )
    input_grad = mixture_back(
        moe_input[0], out_grad[0], routes[0], route_gates[0], up_weight, down_weight
    )
    return (query_grad[None], key_grad[None], value_grad[None], input_grad[None])


def solution(mesh):
    rows = P("exp", "ctx", None)
    experts = P("exp", None, None)
    return jax.shard_map(
        per_device,
        mesh=mesh,
        in_specs=(rows,) * 7 + (experts,) * 2,
        out_specs=(rows,) * 4,
        check_vma=False,
    )
```

time: 369 us -> 203 us (0.55); the launches traced: 364 us -> 203 us
  waiting for transfers between devices: 183 us -> 97.8 us
  local copies, waits for them, and re-layouts: 74.3 us -> 4.83 us
  Pallas kernels: 0 us -> 56.7 us
  matrix products: 40.6 us -> 0 us
  other arithmetic: 22.4 us -> 3.01 us
  starting transfers between devices: 41.9 us -> 25.3 us
  blocking collectives: 0 us -> 14.4 us
    all_to_all x10 -> x0, waiting for transfers between devices: 183 us -> none  [the longest x1 67.3 us: mixture_back(): lax.all_to_all(gated_send, 'exp', split_axis=0, concat_axis=0, tiled=True)]
    ppermute x0 -> x27, waiting for transfers between devices: none -> 97.8 us  [the longest x9 86.5 us: hop(): lax.ppermute(block, 'exp', [(i, (i + 2 * step) % members) for i in range(...]
    pallas_call x0 -> x6, Pallas kernels: none -> 56.7 us  [the longest x3 47.8 us: expert_back(): pl.pallas_call(functools.partial(expert_kernel, sources, top), grid=(expe...]
    all_to_all x10 -> x0, starting transfers between devices: 41.9 us -> none  [the longest x1 5.29 us: attention_back(): lax.all_to_all(split_heads(key_rows), 'ctx', split_axis=2, concat_axis=1,...]
    dot_general x6 -> x0, matrix products: 37.1 us -> none  [the longest x1 17 us: expert_tail(): jnp.einsum('sjkf,jdf->sjkd', hidden_grad, up_weight, preferred_element_ty...]
    unnamed x45 -> x12, local copies, waits for them, and re-layouts: 32 us -> 4.17 us
    ppermute x0 -> x27, starting transfers between devices: none -> 25.3 us  [the longest x9 16.5 us: hop(): lax.ppermute(block, 'exp', [(i, (i + 2 * step) % members) for i in range(...]
    gather x4 -> x1, local copies, waits for them, and re-layouts: 15.1 us -> 0.55 us  [mixture_back(): metas = metas[order]]
  transfers between devices with their start and end apart: 10 -> 27, of which waited for: 8 -> 9; matrix products, arithmetic and copies ran while one was open for 29% -> 1% of each run, Pallas kernels for 0% -> 28%
where the time goes in v1:
time: 203 us
  waiting for transfers between devices  97.8 us (48%)
  Pallas kernels  56.7 us (28%)
  starting transfers between devices  25.3 us (12%)
  blocking collectives  14.4 us (7%)
  local copies, waits for them, and re-layouts  4.83 us (2%)
  other arithmetic  3.01 us (1%)
    ppermute x9, waiting for transfers between devices, hop(): lax.ppermute(block, 'exp', [(i, (i + 2 * step) % members) for i in range(...  86.5 us
    pallas_call x3, Pallas kernels, expert_back(): pl.pallas_call(functools.partial(expert_kernel, sources, top), grid=(expe...  47.8 us
    ppermute x9, starting transfers between devices, hop(): lax.ppermute(block, 'exp', [(i, (i + 2 * step) % members) for i in range(...  16.5 us
    all_gather x1, blocking collectives, mixture_back(): metas = lax.all_gather(meta, 'exp')  14.4 us
    ppermute x6, waiting for transfers between devices, exchange(): return lax.ppermute(block, 'ctx', [(i, i ^ place) for i in range(groups)])  11.2 us
    ppermute x6, starting transfers between devices, exchange(): return lax.ppermute(block, 'ctx', [(i, i ^ place) for i in range(groups)])  7.11 us
    pallas_call x1, Pallas kernels, heads_back(): pl.pallas_call(heads_kernel, grid=(heads,), out_shape=[jax.ShapeDtypeStru...  6.37 us
    unnamed x12, local copies, waits for them, and re-layouts  4.17 us
  transfers between devices with their start and end apart: 27, of which 9 were waited for; matrix products, arithmetic and copies ran while one was open for 1% of the time, Pallas kernels for 28%

profile of v1, /device:TPU:0, one launch (start us, length us, event | category | flops | bytes accessed | tf_op | source)
XLA Modules:
  0.0 202.9 jit_solution(623667100865891728)
XLA Ops:
  0.6 5.1 %collective-permute-start.15 = (bf16[128,2048]{1,0:T(8,128)(2,1)}, bf16[128,2048]{1,0:T(8,128)(2,1)S(1)}, u32[]{:S(2)}, u32[]{:S(2)}) collective-permute-start(bf16[128,2048]{1,0:T(8,128)(2,1)} %bitcast.32), channel_id=1, source_target_pairs={{0,6},{1,7},{2,0},{3,1},{4,2},{5,3},{6,4},{7,5},{8,14},{9,15},{10,... | collective-permute-start | bytes 1572872 | tf_op jit(solution)/shard_map/ppermute | solution.py:251
  5.7 3.9 %collective-permute-start.11 = (bf16[128,2048]{1,0:T(8,128)(2,1)}, bf16[128,2048]{1,0:T(8,128)(2,1)S(1)}, u32[]{:S(2)}, u32[]{:S(2)}) collective-permute-start(bf16[128,2048]{1,0:T(8,128)(2,1)} %bitcast.41), channel_id=1, source_target_pairs={{0,6},{1,7},{2,0},{3,1},{4,2},{5,3},{6,4},{7,5},{8,14},{9,15},{10,... | collective-permute-start | bytes 1572872 | tf_op jit(solution)/shard_map/ppermute | solution.py:251
  9.6 0.1 stack.55
  9.7 8.7 %collective-permute-done.15.refs_6_ = bf16[128,2048]{1,0:T(8,128)(2,1)S(1)} collective-permute-done((bf16[128,2048]{1,0:T(8,128)(2,1)}, bf16[128,2048]{1,0:T(8,128)(2,1)S(1)}, u32[]{:S(2)}, u32[]{:S(2)}) %collective-permute-start.15) | collective-permute-done | bytes 524320 | tf_op jit(solution)/shard_map/ppermute | solution.py:251
  18.4 12.2 %collective-permute-done.9.refs_0_ = bf16[128,2048]{1,0:T(8,128)(2,1)S(1)} collective-permute-done((bf16[128,2048]{1,0:T(8,128)(2,1)}, bf16[128,2048]{1,0:T(8,128)(2,1)S(1)}, u32[]{:S(2)}, u32[]{:S(2)}) %collective-permute-start.9) | collective-permute-done | bytes 524320 | tf_op jit(solution)/shard_map/ppermute | solution.py:251
  30.6 0.0 collective-permute-start.16
  30.6 0.7 convert_bitcast_fusion
  31.3 10.4 %collective-permute-done.13.refs_4_ = bf16[128,2048]{1,0:T(8,128)(2,1)S(1)} collective-permute-done((bf16[128,2048]{1,0:T(8,128)(2,1)}, bf16[128,2048]{1,0:T(8,128)(2,1)S(1)}, u32[]{:S(2)}, u32[]{:S(2)}) %collective-permute-start.13) | collective-permute-done | bytes 524320 | tf_op jit(solution)/shard_map/ppermute | solution.py:251
  41.7 9.3 %collective-permute-done.11.refs_2_ = bf16[128,2048]{1,0:T(8,128)(2,1)S(1)} collective-permute-done((bf16[128,2048]{1,0:T(8,128)(2,1)}, bf16[128,2048]{1,0:T(8,128)(2,1)S(1)}, u32[]{:S(2)}, u32[]{:S(2)}) %collective-permute-start.11) | collective-permute-done | bytes 524320 | tf_op jit(solution)/shard_map/ppermute | solution.py:251
  51.0 0.0 collective-permute-start.14
  51.0 0.0 collective-permute-done.7.refs_3_
  51.0 0.5 collective-permute-start.12
  51.5 0.7 pad_maximum_fusion
  52.2 14.4 %all-gather = f32[64,128]{1,0:T(8,128)S(1)} all-gather(f32[8,128]{1,0:T(8,128)S(1)} %pad_maximum_fusion), channel_id=2, replica_groups=mesh['ctx'=4,'exp'=8] {'exp'}, dimensions={0}, use_global_device_ids=true | all-gather | bytes 36864 | tf_op jit(solution)/shard_map/all_gather | solution.py:262
  66.6 3.8 %collective-permute-start.23 = (bf16[128,2048]{1,0:T(8,128)(2,1)S(1)}, bf16[128,2048]{1,0:T(8,128)(2,1)}, u32[]{:S(2)}, u32[]{:S(2)}) collective-permute-start(bf16[128,2048]{1,0:T(8,128)(2,1)S(1)} %collective-permute-done.15.refs_6_), channel_id=1, source_target_pairs={{0,6},{1,7},{2,0},{3,1},{4,2},{5,3},{6,4},{7,5},{8,14},{9,15},{10,... | collective-permute-start | bytes 1572872 | tf_op jit(solution)/shard_map/ppermute | solution.py:251
  70.4 0.6 gather_fusion
  71.0 0.1 pad_add_fusion.group_ref
  71.1 1.0 copy-done
  72.1 1.0 copy-done.2
  73.1 1.0 copy-done.3
  74.2 1.0 copy-done.4
  75.2 0.7 pack_groups.1
  75.9 1.6 collective-permute-start
  77.5 1.5 collective-permute-start.1
  79.0 0.5 collective-permute-start.2
  79.5 3.2 %collective-permute-done.23.refs_2_ = bf16[128,2048]{1,0:T(8,128)(2,1)} collective-permute-done((bf16[128,2048]{1,0:T(8,128)(2,1)S(1)}, bf16[128,2048]{1,0:T(8,128)(2,1)}, u32[]{:S(2)}, u32[]{:S(2)}) %collective-permute-start.23) | collective-permute-done | bytes 524320 | tf_op jit(solution)/shard_map/ppermute | solution.py:251
  82.7 11.4 %collective-permute-done.21.refs_0_ = bf16[128,2048]{1,0:T(8,128)(2,1)} collective-permute-done((bf16[128,2048]{1,0:T(8,128)(2,1)S(1)}, bf16[128,2048]{1,0:T(8,128)(2,1)}, u32[]{:S(2)}, u32[]{:S(2)}) %collective-permute-start.21) | collective-permute-done | bytes 524320 | tf_op jit(solution)/shard_map/ppermute | solution.py:251
  94.1 17.5 %expert_back.4 = (f32[128,2048]{1,0:T(8,128)S(1)}, bf16[128,2048]{1,0:T(8,128)(2,1)S(1)}, f32[128,2048]{1,0:T(8,128)S(1)}, bf16[128,2048]{1,0:T(8,128)(2,1)S(1)}) custom-call(f32[4,8,128]{2,1,0:T(8,128)S(1)} %slice.41.meta_ref, bf16[128,2048]{1,0:T(8,128)(2,1)S(1)} %collective-permute-done.9.refs_0_, bf16[128,2048]{1,0:T(8,128)(2,1)S(1)} %collective-permute-done.10.refs_1_, ...), custom_call_target="tpu_custom_call" | custom-call | flops 3623878656 | bytes 33554432 | tf_op jit(solution)/shard_map/expert_back/pallas_call | solution.py:210
  111.6 0.6 collective-permute-start.17
  112.2 15.2 %expert_back.3 = (f32[128,2048]{1,0:T(8,128)S(1)}, bf16[128,2048]{1,0:T(8,128)(2,1)S(1)}) custom-call(f32[2,8,128]{2,1,0:T(8,128)S(1)} %get-tuple-element.54.meta_ref, bf16[128,2048]{1,0:T(8,128)(2,1)S(1)} %bitcast.43, bf16[128,2048]{1,0:T(8,128)(2,1)} %collective-permute-done.6.refs_1_, bf16[128,2048]{1,0:T(8,128)(2,1)S(1)} %bitcast.36, ...), custom_call_target="tpu_custom_call" | custom-call | flops 1811939328 | bytes 29360128 | tf_op jit(solution)/shard_map/expert_back/pallas_call | solution.py:210
  127.4 0.1 collective-permute-start.8
  127.5 6.4 %heads_back.1 = (bf16[3,128,512]{2,1,0:T(8,128)(2,1)S(1)}, bf16[3,128,512]{2,1,0:T(8,128)(2,1)S(1)}, bf16[3,128,512]{2,1,0:T(8,128)(2,1)S(1)}, bf16[3,128,512]{2,1,0:T(8,128)(2,1)S(1)}) custom-call(bf16[4,128,512]{2,1,0:T(8,128)(2,1)S(1)} %get-tuple-element.35.refs_0_, bf16[4,128,512]{2,1,0:T(8,128)(2,1)S(1)} %collective-permute-done.refs_1_, ...), custom_call_target="tpu_custom_call" | custom-call | flops 2684354560 | bytes 3670016 | tf_op jit(solution)/shard_map/heads_back/pallas_call | solution.py:117
  133.9 1.6 collective-permute-start.3
  135.4 1.5 collective-permute-start.4
  137.0 15.2 %expert_back.5 = (f32[128,2048]{1,0:T(8,128)S(1)}, bf16[128,2048]{1,0:T(8,128)(2,1)S(1)}) custom-call(f32[2,8,128]{2,1,0:T(8,128)S(1)} %get-tuple-element.55.meta_ref, bf16[128,2048]{1,0:T(8,128)(2,1)} %collective-permute-done.21.refs_0_, bf16[128,2048]{1,0:T(8,128)(2,1)S(1)} %collective-permute-done.22.refs_1_, ...), custom_call_target="tpu_custom_call" | custom-call | flops 1811939328 | bytes 29360128 | tf_op jit(solution)/shard_map/expert_back/pallas_call | solution.py:210
  152.2 0.6 collective-permute-start.25
  152.7 0.1 add_convert_fusion.3
  152.9 1.9 collective-permute-start.18
  154.7 0.1 add_convert_fusion.2
  154.9 1.2 collective-permute-start.20
  156.1 0.1 add_convert_fusion.1
  156.2 0.7 collective-permute-start.26
  156.9 0.5 collective-permute-start.5
  157.3 11.2 %collective-permute-done.5.refs_3_ = bf16[3,128,512]{2,1,0:T(8,128)(2,1)S(1)} collective-permute-done((bf16[3,128,512]{2,1,0:T(8,128)(2,1)S(1)}, bf16[3,128,512]{2,1,0:T(8,128)(2,1)S(1)}, u32[]{:S(2)}, u32[]{:S(2)}) %collective-permute-start.5) | collective-permute-done | bytes 393248 | tf_op jit(solution)/shard_map/ppermute | solution.py:141
  168.6 1.8 unpack_groups.1
  170.4 9.2 %collective-permute-done.20 = bf16[128,2048]{1,0:T(8,128)(2,1)S(1)} collective-permute-done((bf16[128,2048]{1,0:T(8,128)(2,1)S(1)}, bf16[128,2048]{1,0:T(8,128)(2,1)S(1)}, u32[]{:S(2)}, u32[]{:S(2)}) %collective-permute-start.20) | collective-permute-done | bytes 524320 | tf_op jit(solution)/shard_map/ppermute | solution.py:251
  179.6 22.1 %collective-permute-done.26 = bf16[128,2048]{1,0:T(8,128)(2,1)S(1)} collective-permute-done((bf16[128,2048]{1,0:T(8,128)(2,1)S(1)}, bf16[128,2048]{1,0:T(8,128)(2,1)S(1)}, u32[]{:S(2)}, u32[]{:S(2)}) %collective-permute-start.26) | collective-permute-done | bytes 524320 | tf_op jit(solution)/shard_map/ppermute | solution.py:251
  201.7 1.2 fusion
  (39 shorter events, 0.1 us)
Async XLA Ops:
  0.6 17.7 %collective-permute-start.15 = (bf16[128,2048]{1,0:T(8,128)(2,1)}, bf16[128,2048]{1,0:T(8,128)(2,1)S(1)}, u32[]{:S(2)}, u32[]{:S(2)}) collective-permute-start(bf16[128,2048]{1,0:T(8,128)(2,1)} %bitcast.32), channel_id=1, source_target_pairs={{0,6},{1,7},{2,0},{3,1},{4,2},{5,3},{6,4},{7,5},{8,14},{9,15},{10,... | collective-permute-start | bytes 1572872 | tf_op jit(solution)/shard_map/ppermute | solution.py:251
  5.7 24.8 %collective-permute-start.9 = (bf16[128,2048]{1,0:T(8,128)(2,1)}, bf16[128,2048]{1,0:T(8,128)(2,1)S(1)}, u32[]{:S(2)}, u32[]{:S(2)}) collective-permute-start(bf16[128,2048]{1,0:T(8,128)(2,1)} %bitcast.40), channel_id=1, source_target_pairs={{0,2},{1,3},{2,4},{3,5},{4,6},{5,7},{6,0},{7,1},{8,10},{9,11},{10,... | collective-permute-start | bytes 1572872 | tf_op jit(solution)/shard_map/ppermute | solution.py:251
  5.7 36.0 %collective-permute-start.13 = (bf16[128,2048]{1,0:T(8,128)(2,1)}, bf16[128,2048]{1,0:T(8,128)(2,1)S(1)}, u32[]{:S(2)}, u32[]{:S(2)}) collective-permute-start(bf16[128,2048]{1,0:T(8,128)(2,1)} %bitcast.33), channel_id=1, source_target_pairs={{0,2},{1,3},{2,4},{3,5},{4,6},{5,7},{6,0},{7,1},{8,10},{9,11},{10,... | collective-permute-start | bytes 1572872 | tf_op jit(solution)/shard_map/ppermute | solution.py:251
  5.7 45.2 %collective-permute-start.11 = (bf16[128,2048]{1,0:T(8,128)(2,1)}, bf16[128,2048]{1,0:T(8,128)(2,1)S(1)}, u32[]{:S(2)}, u32[]{:S(2)}) collective-permute-start(bf16[128,2048]{1,0:T(8,128)(2,1)} %bitcast.41), channel_id=1, source_target_pairs={{0,6},{1,7},{2,0},{3,1},{4,2},{5,3},{6,4},{7,5},{8,14},{9,15},{10,... | collective-permute-start | bytes 1572872 | tf_op jit(solution)/shard_map/ppermute | solution.py:251
  9.6 41.4 %collective-permute-start.7 = (bf16[128,2048]{1,0:T(8,128)(2,1)}, bf16[128,2048]{1,0:T(8,128)(2,1)}, u32[]{:S(2)}, u32[]{:S(2)}) collective-permute-start(bf16[128,2048]{1,0:T(8,128)(2,1)} %bitcast.34), channel_id=1, source_target_pairs={{0,1},{1,0},{2,3},{3,2},{4,5},{5,4},{6,7},{7,6},{8,9},{9,8},{10,11... | collective-permute-start | bytes 1572872 | tf_op jit(solution)/shard_map/ppermute | solution.py:248
  18.4 48.2 %collective-permute-start.6 = (bf16[128,2048]{1,0:T(8,128)(2,1)}, bf16[128,2048]{1,0:T(8,128)(2,1)}, u32[]{:S(2)}, u32[]{:S(2)}) collective-permute-start(bf16[128,2048]{1,0:T(8,128)(2,1)} %bitcast.42), channel_id=1, source_target_pairs={{0,1},{1,0},{2,3},{3,2},{4,5},{5,4},{6,7},{7,6},{8,9},{9,8},{10,11... | collective-permute-start | bytes 1572872 | tf_op jit(solution)/shard_map/ppermute | solution.py:248
  30.6 39.8 %collective-permute-start.16 = (bf16[128,2048]{1,0:T(8,128)(2,1)S(1)}, bf16[128,2048]{1,0:T(8,128)(2,1)S(1)}, u32[]{:S(2)}, u32[]{:S(2)}) collective-permute-start(bf16[128,2048]{1,0:T(8,128)(2,1)S(1)} %collective-permute-done.15.refs_6_), channel_id=1, source_target_pairs={{0,1},{1,0},{2,3},{3,2},{4,5},{5,4},{6,7},{7,6},{8,9},{9,8},{10,11... | collective-permute-start | bytes 1572872 | tf_op jit(solution)/shard_map/ppermute | solution.py:248
  41.7 34.2 %collective-permute-start.10 = (bf16[128,2048]{1,0:T(8,128)(2,1)S(1)}, bf16[128,2048]{1,0:T(8,128)(2,1)S(1)}, u32[]{:S(2)}, u32[]{:S(2)}) collective-permute-start(bf16[128,2048]{1,0:T(8,128)(2,1)S(1)} %collective-permute-done.9.refs_0_), channel_id=1, source_target_pairs={{0,1},{1,0},{2,3},{3,2},{4,5},{5,4},{6,7},{7,6},{8,9},{9,8},{10,11... | collective-permute-start | bytes 1572872 | tf_op jit(solution)/shard_map/ppermute | solution.py:248
  51.0 26.5 %collective-permute-start.14 = (bf16[128,2048]{1,0:T(8,128)(2,1)S(1)}, bf16[128,2048]{1,0:T(8,128)(2,1)}, u32[]{:S(2)}, u32[]{:S(2)}) collective-permute-start(bf16[128,2048]{1,0:T(8,128)(2,1)S(1)} %collective-permute-done.13.refs_4_), channel_id=1, source_target_pairs={{0,1},{1,0},{2,3},{3,2},{4,5},{5,4},{6,7},{7,6},{8,9},{9,8},{10,11... | collective-permute-start | bytes 1572872 | tf_op jit(solution)/shard_map/ppermute | solution.py:248
  51.0 28.0 %collective-permute-start.12 = (bf16[128,2048]{1,0:T(8,128)(2,1)S(1)}, bf16[128,2048]{1,0:T(8,128)(2,1)}, u32[]{:S(2)}, u32[]{:S(2)}) collective-permute-start(bf16[128,2048]{1,0:T(8,128)(2,1)S(1)} %collective-permute-done.11.refs_2_), channel_id=1, source_target_pairs={{0,1},{1,0},{2,3},{3,2},{4,5},{5,4},{6,7},{7,6},{8,9},{9,8},{10,11... | collective-permute-start | bytes 1572872 | tf_op jit(solution)/shard_map/ppermute | solution.py:248
  66.6 16.1 %collective-permute-start.23 = (bf16[128,2048]{1,0:T(8,128)(2,1)S(1)}, bf16[128,2048]{1,0:T(8,128)(2,1)}, u32[]{:S(2)}, u32[]{:S(2)}) collective-permute-start(bf16[128,2048]{1,0:T(8,128)(2,1)S(1)} %collective-permute-done.15.refs_6_), channel_id=1, source_target_pairs={{0,6},{1,7},{2,0},{3,1},{4,2},{5,3},{6,4},{7,5},{8,14},{9,15},{10,... | collective-permute-start | bytes 1572872 | tf_op jit(solution)/shard_map/ppermute | solution.py:251
  70.4 23.7 %collective-permute-start.21 = (bf16[128,2048]{1,0:T(8,128)(2,1)S(1)}, bf16[128,2048]{1,0:T(8,128)(2,1)}, u32[]{:S(2)}, u32[]{:S(2)}) collective-permute-start(bf16[128,2048]{1,0:T(8,128)(2,1)S(1)} %collective-permute-done.9.refs_0_), channel_id=1, source_target_pairs={{0,2},{1,3},{2,4},{3,5},{4,6},{5,7},{6,0},{7,1},{8,10},{9,11},{10,... | collective-permute-start | bytes 1572872 | tf_op jit(solution)/shard_map/ppermute | solution.py:251
  71.1 1.0 copy-start
  72.1 1.0 copy-start.2
  73.1 1.0 copy-start.3
  74.2 1.0 copy-start.4
  75.9 35.6 %collective-permute-start = (bf16[4,128,512]{2,1,0:T(8,128)(2,1)S(1)}, bf16[4,128,512]{2,1,0:T(8,128)(2,1)S(1)}, u32[]{:S(2)}, u32[]{:S(2)}) collective-permute-start(bf16[4,128,512]{2,1,0:T(8,128)(2,1)S(1)} %get-tuple-element.36), channel_id=1, source_target_pairs={{0,8},{8,0},{16,24},{24,16},{1,9},{9,1},{17,25},{25,17},{2,10},{10... | collective-permute-start | bytes 1572872 | tf_op jit(solution)/shard_map/ppermute | solution.py:141
  77.5 49.9 %collective-permute-start.1 = (bf16[4,128,512]{2,1,0:T(8,128)(2,1)S(1)}, bf16[4,128,512]{2,1,0:T(8,128)(2,1)S(1)}, u32[]{:S(2)}, u32[]{:S(2)}) collective-permute-start(bf16[4,128,512]{2,1,0:T(8,128)(2,1)S(1)} %get-tuple-element.37), channel_id=1, source_target_pairs={{0,16},{8,24},{16,0},{24,8},{1,17},{9,25},{17,1},{25,9},{2,18},{10... | collective-permute-start | bytes 1572872 | tf_op jit(solution)/shard_map/ppermute | solution.py:141
  79.0 48.5 %collective-permute-start.2 = (bf16[4,128,512]{2,1,0:T(8,128)(2,1)S(1)}, bf16[4,128,512]{2,1,0:T(8,128)(2,1)S(1)}, u32[]{:S(2)}, u32[]{:S(2)}) collective-permute-start(bf16[4,128,512]{2,1,0:T(8,128)(2,1)S(1)} %get-tuple-element.38), channel_id=1, source_target_pairs={{0,24},{8,16},{16,8},{24,0},{1,25},{9,17},{17,9},{25,1},{2,26},{10... | collective-permute-start | bytes 1572872 | tf_op jit(solution)/shard_map/ppermute | solution.py:141
  79.5 32.7 %copy-start.1 = (bf16[1,128,2048]{2,1,0:T(8,128)(2,1)S(1)}, bf16[1,128,2048]{2,1,0:T(8,128)(2,1)}, u32[]{:S(2)}) copy-start(bf16[1,128,2048]{2,1,0:T(8,128)(2,1)} %param.14) | copy-start | bytes 1572868
  79.5 32.7 %copy-start.5 = (bf16[1,128,2048]{2,1,0:T(8,128)(2,1)S(1)}, bf16[1,128,2048]{2,1,0:T(8,128)(2,1)}, u32[]{:S(2)}) copy-start(bf16[1,128,2048]{2,1,0:T(8,128)(2,1)} %param.15) | copy-start | bytes 1572868
  82.7 52.7 %collective-permute-start.24 = (bf16[128,2048]{1,0:T(8,128)(2,1)}, bf16[128,2048]{1,0:T(8,128)(2,1)S(1)}, u32[]{:S(2)}, u32[]{:S(2)}) collective-permute-start(bf16[128,2048]{1,0:T(8,128)(2,1)} %collective-permute-done.23.refs_2_), channel_id=1, source_target_pairs={{0,1},{1,0},{2,3},{3,2},{4,5},{5,4},{6,7},{7,6},{8,9},{9,8},{10,11... | collective-permute-start | bytes 1572872 | tf_op jit(solution)/shard_map/ppermute | solution.py:248
  94.1 42.8 %collective-permute-start.22 = (bf16[128,2048]{1,0:T(8,128)(2,1)}, bf16[128,2048]{1,0:T(8,128)(2,1)S(1)}, u32[]{:S(2)}, u32[]{:S(2)}) collective-permute-start(bf16[128,2048]{1,0:T(8,128)(2,1)} %collective-permute-done.21.refs_0_), channel_id=1, source_target_pairs={{0,1},{1,0},{2,3},{3,2},{4,5},{5,4},{6,7},{7,6},{8,9},{9,8},{10,11... | collective-permute-start | bytes 1572872 | tf_op jit(solution)/shard_map/ppermute | solution.py:248
  111.6 40.6 %collective-permute-start.17 = (bf16[128,2048]{1,0:T(8,128)(2,1)S(1)}, bf16[128,2048]{1,0:T(8,128)(2,1)S(1)}, u32[]{:S(2)}, u32[]{:S(2)}) collective-permute-start(bf16[128,2048]{1,0:T(8,128)(2,1)S(1)} %get-tuple-element.49), channel_id=1, source_target_pairs={{0,1},{1,0},{2,3},{3,2},{4,5},{5,4},{6,7},{7,6},{8,9},{9,8},{10,11... | collective-permute-start | bytes 1572872 | tf_op jit(solution)/shard_map/ppermute | solution.py:248
  127.4 43.0 %collective-permute-start.8 = (bf16[128,2048]{1,0:T(8,128)(2,1)S(1)}, bf16[128,2048]{1,0:T(8,128)(2,1)S(1)}, u32[]{:S(2)}, u32[]{:S(2)}) collective-permute-start(bf16[128,2048]{1,0:T(8,128)(2,1)S(1)} %get-tuple-element.47), channel_id=1, source_target_pairs={{0,1},{1,0},{2,3},{3,2},{4,5},{5,4},{6,7},{7,6},{8,9},{9,8},{10,11... | collective-permute-start | bytes 1572872 | tf_op jit(solution)/shard_map/ppermute | solution.py:248
  133.9 22.3 %collective-permute-start.3 = (bf16[3,128,512]{2,1,0:T(8,128)(2,1)S(1)}, bf16[3,128,512]{2,1,0:T(8,128)(2,1)S(1)}, u32[]{:S(2)}, u32[]{:S(2)}) collective-permute-start(bf16[3,128,512]{2,1,0:T(8,128)(2,1)S(1)} %get-tuple-element.40), channel_id=1, source_target_pairs={{0,8},{8,0},{16,24},{24,16},{1,9},{9,1},{17,25},{25,17},{2,10},{10... | collective-permute-start | bytes 1179656 | tf_op jit(solution)/shard_map/ppermute | solution.py:141
  135.4 21.4 %collective-permute-start.4 = (bf16[3,128,512]{2,1,0:T(8,128)(2,1)S(1)}, bf16[3,128,512]{2,1,0:T(8,128)(2,1)S(1)}, u32[]{:S(2)}, u32[]{:S(2)}) collective-permute-start(bf16[3,128,512]{2,1,0:T(8,128)(2,1)S(1)} %get-tuple-element.41), channel_id=1, source_target_pairs={{0,16},{8,24},{16,0},{24,8},{1,17},{9,25},{17,1},{25,9},{2,18},{10... | collective-permute-start | bytes 1179656 | tf_op jit(solution)/shard_map/ppermute | solution.py:141
  137.0 15.9 %collective-permute-start.19 = (bf16[128,2048]{1,0:T(8,128)(2,1)S(1)}, bf16[128,2048]{1,0:T(8,128)(2,1)S(1)}, u32[]{:S(2)}, u32[]{:S(2)}) collective-permute-start(bf16[128,2048]{1,0:T(8,128)(2,1)S(1)} %get-tuple-element.51), channel_id=1, source_target_pairs={{0,1},{1,0},{2,3},{3,2},{4,5},{5,4},{6,7},{7,6},{8,9},{9,8},{10,11... | collective-permute-start | bytes 1572872 | tf_op jit(solution)/shard_map/ppermute | solution.py:248
  152.2 2.7 %collective-permute-start.25 = (bf16[128,2048]{1,0:T(8,128)(2,1)S(1)}, bf16[128,2048]{1,0:T(8,128)(2,1)S(1)}, u32[]{:S(2)}, u32[]{:S(2)}) collective-permute-start(bf16[128,2048]{1,0:T(8,128)(2,1)S(1)} %get-tuple-element.53), channel_id=1, source_target_pairs={{0,1},{1,0},{2,3},{3,2},{4,5},{5,4},{6,7},{7,6},{8,9},{9,8},{10,11... | collective-permute-start | bytes 1572872 | tf_op jit(solution)/shard_map/ppermute | solution.py:248
  152.9 17.5 %collective-permute-start.18 = (bf16[128,2048]{1,0:T(8,128)(2,1)S(1)}, bf16[128,2048]{1,0:T(8,128)(2,1)S(1)}, u32[]{:S(2)}, u32[]{:S(2)}) collective-permute-start(bf16[128,2048]{1,0:T(8,128)(2,1)S(1)} %add_convert_fusion.3), channel_id=1, source_target_pairs={{0,6},{1,7},{2,0},{3,1},{4,2},{5,3},{6,4},{7,5},{8,14},{9,15},{10,... | collective-permute-start | bytes 1572872 | tf_op jit(solution)/shard_map/ppermute | solution.py:251
  154.9 24.7 %collective-permute-start.20 = (bf16[128,2048]{1,0:T(8,128)(2,1)S(1)}, bf16[128,2048]{1,0:T(8,128)(2,1)S(1)}, u32[]{:S(2)}, u32[]{:S(2)}) collective-permute-start(bf16[128,2048]{1,0:T(8,128)(2,1)S(1)} %add_convert_fusion.2), channel_id=1, source_target_pairs={{0,2},{1,3},{2,4},{3,5},{4,6},{5,7},{6,0},{7,1},{8,10},{9,11},{10,... | collective-permute-start | bytes 1572872 | tf_op jit(solution)/shard_map/ppermute | solution.py:251
  156.2 45.5 %collective-permute-start.26 = (bf16[128,2048]{1,0:T(8,128)(2,1)S(1)}, bf16[128,2048]{1,0:T(8,128)(2,1)S(1)}, u32[]{:S(2)}, u32[]{:S(2)}) collective-permute-start(bf16[128,2048]{1,0:T(8,128)(2,1)S(1)} %add_convert_fusion.1), channel_id=1, source_target_pairs={{0,4},{1,5},{2,6},{3,7},{4,0},{5,1},{6,2},{7,3},{8,12},{9,13},{10,... | collective-permute-start | bytes 1572872 | tf_op jit(solution)/shard_map/ppermute | solution.py:251
  156.9 11.7 %collective-permute-start.5 = (bf16[3,128,512]{2,1,0:T(8,128)(2,1)S(1)}, bf16[3,128,512]{2,1,0:T(8,128)(2,1)S(1)}, u32[]{:S(2)}, u32[]{:S(2)}) collective-permute-start(bf16[3,128,512]{2,1,0:T(8,128)(2,1)S(1)} %get-tuple-element.42), channel_id=1, source_target_pairs={{0,24},{8,16},{16,8},{24,0},{1,25},{9,17},{17,9},{25,1},{2,26},{10... | collective-permute-start | bytes 1179656 | tf_op jit(solution)/shard_map/ppermute | solution.py:141

commit v2 on v1

v2 whole, which is shorter than its diff:
```python
import functools

import jax
import jax.numpy as jnp
from jax import lax
from jax.experimental import pallas as pl
from jax.experimental.pallas import tpu as pltpu
from jax.sharding import PartitionSpec as P

HD = 128
CAP = 24
NOTES = 16
VMEM_BYTES = 44 * 1024 * 1024
NT = (((1,), (1,)), ((), ()))
TN = (((0,), (0,)), ((), ()))


def dot_nt(left, right):
    return lax.dot_general(left, right, NT, preferred_element_type=jnp.float32)


def dot_tn(left, right):
    return lax.dot_general(left, right, TN, preferred_element_type=jnp.float32)


def dot_nn(left, right):
    return jnp.dot(left, right, preferred_element_type=jnp.float32)


def silu_slope(preact):
    sigmoid = jax.nn.sigmoid(preact)
    return sigmoid * (1.0 + preact * (1.0 - sigmoid))


def pack_kernel(*refs):
    *members, packed = refs
    groups, _, _, width = packed.shape
    for group in range(groups):
        for row, member in enumerate(members):
            packed[group, row] = member[:, group * width : (group + 1) * width]


def pack_groups(members, groups):
    bins, width = members[0].shape
    return pl.pallas_call(
        pack_kernel,
        out_shape=jax.ShapeDtypeStruct((groups, 4, bins, width // groups), jnp.bfloat16),
        compiler_params=pltpu.CompilerParams(vmem_limit_bytes=VMEM_BYTES),
        cost_estimate=pl.CostEstimate(
            flops=0, bytes_accessed=16 * bins * width, transcendentals=0
        ),
        name="pack_groups",
    )(*members)


def unpack_kernel(packed, *outs):
    groups, _, _, width = packed.shape
    for group in range(groups):
        for row, out in enumerate(outs):
            out[:, group * width : (group + 1) * width] = packed[group, row]


def unpack_groups(packed):
    groups, count, bins, width = packed.shape
    out = jax.ShapeDtypeStruct((bins, width * groups), jnp.bfloat16)
    return pl.pallas_call(
        unpack_kernel,
        out_shape=[out] * count,
        compiler_params=pltpu.CompilerParams(vmem_limit_bytes=VMEM_BYTES),
        cost_estimate=pl.CostEstimate(
            flops=0, bytes_accessed=12 * bins * width * groups, transcendentals=0
        ),
        name="unpack_groups",
    )(packed)


def heads_kernel(packed, out):
    groups, _, bins, _ = packed.shape
    rows = groups * bins
    scale = HD ** (-0.5)
    query, key, value, grad = (packed[:, row].reshape(rows, HD) for row in range(4))
    scores = dot_nt(key, query) * scale
    powers = jnp.exp(scores - jnp.max(scores, axis=0, keepdims=True))
    probs = powers * (1.0 / jnp.sum(powers, axis=0, keepdims=True))
    prob_grad = dot_nt(value, grad)
    row_delta = jnp.sum(probs * prob_grad, axis=0, keepdims=True)
    score_grad = (probs * (prob_grad - row_delta)).astype(jnp.bfloat16)
    results = (
        dot_tn(score_grad, key) * scale,
        dot_nn(score_grad, query) * scale,
        dot_nn(probs.astype(jnp.bfloat16), grad),
    )
    for row, result in enumerate(results):
        out[:, row] = result.astype(jnp.bfloat16).reshape(groups, bins, HD)


def heads_back(packed):
    groups, _, bins, width = packed.shape
    rows = bins * groups
    heads = width // HD
    return pl.pallas_call(
        heads_kernel,
        grid=(heads,),
        out_shape=jax.ShapeDtypeStruct((groups, 3, bins, width), jnp.bfloat16),
        in_specs=[pl.BlockSpec((groups, 4, bins, HD), lambda h: (0, 0, 0, h))],
        out_specs=pl.BlockSpec((groups, 3, bins, HD), lambda h: (0, 0, 0, h)),
        compiler_params=pltpu.CompilerParams(vmem_limit_bytes=VMEM_BYTES),
        cost_estimate=pl.CostEstimate(
            flops=20 * heads * rows * rows * HD,
            bytes_accessed=14 * rows * width,
            transcendentals=heads * rows * rows,
        ),
        name="heads_back",
    )(packed)


def exchange(packed):
    return lax.all_to_all(packed, "ctx", split_axis=0, concat_axis=0, tiled=True)


def block_kernel(tokens_ref, grads_ref, routes_ref, gates_ref, block_ref):
    bins, width = tokens_ref.shape
    block_ref[:bins] = tokens_ref[...]
    block_ref[bins : 2 * bins] = grads_ref[...]
    block_ref[2 * bins :] = jnp.zeros((NOTES, width), jnp.bfloat16)
    diagonal = lax.broadcasted_iota(jnp.int32, (bins, bins), 0) == lax.broadcasted_iota(
        jnp.int32, (bins, bins), 1
    )
    diagonal = diagonal.astype(jnp.bfloat16)
    rest = gates_ref[...]
    pieces = [(routes_ref[...] + 1).astype(jnp.float32).astype(jnp.bfloat16)]
    for _ in range(3):
        piece = rest.astype(jnp.bfloat16)
        rest = rest - piece.astype(jnp.float32)
        pieces.append(piece)
    notes = jnp.concatenate([dot_tn(piece, diagonal) for piece in pieces], axis=0)
    block_ref[2 * bins : 2 * bins + notes.shape[0], :bins] = notes.astype(jnp.bfloat16)


def make_block(tokens, grads, routes, gates):
    bins, width = tokens.shape
    return pl.pallas_call(
        block_kernel,
        out_shape=jax.ShapeDtypeStruct((2 * bins + NOTES, width), jnp.bfloat16),
        compiler_params=pltpu.CompilerParams(vmem_limit_bytes=VMEM_BYTES),
        cost_estimate=pl.CostEstimate(
            flops=0, bytes_accessed=8 * bins * width, transcendentals=0
        ),
        name="make_block",
    )(tokens, grads, routes, gates)


def expert_kernel(sources, top, base_ref, *refs):
    block_refs = refs[:sources]
    up_ref, down_ref = refs[sources : sources + 2]
    keep_refs = refs[sources + 2 : -5]
    give_ref, pick_ref, token_rows, gated_rows, back_rows = refs[-5:]
    bins = keep_refs[0].shape[0]
    slots = sources * CAP
    experts = pick_ref.shape[0] // slots
    expert = pl.program_id(0)

    @pl.when(expert == 0)
    def _():
        earlier = lax.broadcasted_iota(jnp.int32, (bins, bins), 0)
        later = lax.broadcasted_iota(jnp.int32, (bins, bins), 1)
        before = (earlier < later).astype(jnp.bfloat16)
        slot = lax.broadcasted_iota(jnp.int32, (slots, bins), 0).astype(jnp.float32)
        base = base_ref[0].astype(jnp.float32)
        gates = [jnp.zeros((slots, 1), jnp.float32)] * experts
        for source, block in enumerate(block_refs):
            notes = block[2 * bins :, :bins].astype(jnp.float32)
            named = notes[:top] - base
            weights = notes[top : 2 * top] + notes[2 * top : 3 * top] + notes[3 * top : 4 * top]
            hits = [(named == float(local + 1)).astype(jnp.float32) for local in range(experts)]
            chosen = [jnp.sum(hit, axis=0, keepdims=True) for hit in hits]
            stacked = jnp.concatenate(chosen, axis=0)
            position = dot_nn(stacked.astype(jnp.bfloat16), before)
            for local in range(experts):
                place = jnp.where(
                    chosen[local] > 0.0, position[local : local + 1] + float(source * CAP), -1.0
                )
                pick = (slot == place).astype(jnp.float32)
                gate = jnp.sum(hits[local] * weights, axis=0, keepdims=True)
                gates[local] = gates[local] + jnp.sum(pick * gate, axis=1, keepdims=True)
                pick_ref[
                    local * slots : (local + 1) * slots, source * bins : (source + 1) * bins
                ] = pick.astype(jnp.bfloat16)
        picks = pick_ref[...]
        tokens = jnp.concatenate([block[:bins] for block in block_refs], axis=0)
        token_rows[...] = dot_nn(picks, tokens).astype(jnp.bfloat16)
        grads = jnp.concatenate([block[bins : 2 * bins] for block in block_refs], axis=0)
        gate_column = jnp.concatenate(gates, axis=0)
        gated_rows[...] = (gate_column * dot_nn(picks, grads)).astype(jnp.bfloat16)

    rows = pl.ds(pl.multiple_of(expert * slots, 16), slots)
    preact = dot_nn(token_rows[rows, :], up_ref[0])
    back_grad = dot_nt(gated_rows[rows, :], down_ref[0])
    hidden_grad = (back_grad * silu_slope(preact)).astype(jnp.bfloat16)
    back_rows[rows, :] = dot_nt(hidden_grad, up_ref[0]).astype(jnp.bfloat16)

    @pl.when(expert == experts - 1)
    def _():
        sums = dot_tn(pick_ref[...], back_rows[...])
        for pair, keep in enumerate(keep_refs):
            mine, other = 2 * pair * bins, (2 * pair + 1) * bins
            keep[...] = sums[mine : mine + bins]
            give_ref[pair * bins : (pair + 1) * bins] = sums[other : other + bins].astype(
                jnp.bfloat16
            )


def expert_back(base, blocks, up_weight, down_weight, bins, top):
    sources = len(blocks)
    experts, width, hidden = up_weight.shape
    slots = sources * CAP
    pairs = sources // 2
    return pl.pallas_call(
        functools.partial(expert_kernel, sources, top),
        grid=(experts,),
        out_shape=[jax.ShapeDtypeStruct((bins, width), jnp.float32)] * pairs
        + [jax.ShapeDtypeStruct((pairs * bins, width), jnp.bfloat16)],
        in_specs=[pl.BlockSpec(memory_space=pltpu.SMEM)]
        + [pl.BlockSpec(block.shape, lambda e: (0, 0)) for block in blocks]
        + [
            pl.BlockSpec((1, width, hidden), lambda e: (e, 0, 0)),
            pl.BlockSpec((1, hidden, width), lambda e: (e, 0, 0)),
        ],
        out_specs=[pl.BlockSpec((bins, width), lambda e: (0, 0))] * pairs
        + [pl.BlockSpec((pairs * bins, width), lambda e: (0, 0))],
        scratch_shapes=[
            pltpu.VMEM((experts * slots, sources * bins), jnp.bfloat16),
            pltpu.VMEM((experts * slots, width), jnp.bfloat16),
            pltpu.VMEM((experts * slots, width), jnp.bfloat16),
            pltpu.VMEM((experts * slots, width), jnp.bfloat16),
        ],
        compiler_params=pltpu.CompilerParams(vmem_limit_bytes=VMEM_BYTES),
        cost_estimate=pl.CostEstimate(
            flops=6 * experts * slots * width * hidden,
            bytes_accessed=4 * experts * width * hidden + 8 * sources * bins * width,
            transcendentals=experts * slots * hidden,
        ),
        name="expert_back",
    )(base, *blocks, up_weight, down_weight)


def per_device(
    queries, key_rows, value_rows, out_grad, moe_input, routes, route_gates, up_weight, down_weight
):
    members = lax.axis_size("exp")
    me = lax.axis_index("exp")
    groups = lax.axis_size("ctx")
    chips = members // 2
    half = chips // 2
    _, bins, top = routes.shape
    base = (me * up_weight.shape[0]).astype(jnp.int32).reshape(1)

    def swap(block):
        return lax.ppermute(block, "exp", [(i, i ^ 1) for i in range(members)])

    def move(block, pairs):
        wide = [(2 * a + core, 2 * b + core) for a, b in pairs for core in range(2)]
        return lax.ppermute(block, "exp", wide)

    def line(distance, sign):
        return [(i, i + sign * distance) for i in range(chips) if 0 <= i + sign * distance < chips]

    def work(*arrivals):
        blocks = []
        for _, _, block in arrivals:
            blocks += [block, swap(block)]
        *kept, give = expert_back(base, blocks, up_weight, down_weight, bins, top)
        return arrivals, kept, swap(give)

    def send_back(arrivals, kept, given):
        parts = []
        for place, (kind, distance, _) in enumerate(arrivals):
            both = kept[place] + given[place * bins : (place + 1) * bins].astype(jnp.float32)
            if distance > 0:
                pairs = []
                if kind != "after":
                    pairs += line(distance, -1)
                if kind != "before":
                    pairs += line(distance, 1)
                both = move(both.astype(jnp.bfloat16), pairs)
            parts.append(both)
        return parts

    own = make_block(moe_input[0], out_grad[0], routes[0], route_gates[0])
    packed = pack_groups((queries[0], key_rows[0], value_rows[0], out_grad[0]), groups)
    heads = exchange(packed)
    parts, results = [], None
    arrivals, kept, given = work(("own", 0, own))
    right, left = own, own
    for d in range(1, half + 1):
        right = move(right, [(i, i + 1) for i in range(d - 1, chips - 1)])
        left = move(left, [(i, i - 1) for i in range(1, chips - d + 1)])
        right, left, kept, results = lax.optimization_barrier((right, left, kept, results))
        parts += send_back(arrivals, kept, given)
        arrivals = []
        if results is None:
            results = heads_back(heads)
        if d < half:
            arrivals, kept, given = work(("before", d, right), ("after", d, left))
    far = jnp.where(me >= 2 * half, right, left)
    outs = unpack_groups(exchange(results))
    for d in range(half, chips):
        if d > half:
            inward = [(i - 1, i) for i in range(d, chips)] + [(i + 1, i) for i in range(chips - d)]
            far, kept, given, parts, outs = lax.optimization_barrier(
                (move(far, inward), kept, given, parts, outs)
            )
            parts += send_back(arrivals, kept, given)
        arrivals, kept, given = work(("far", d, far))
    parts += send_back(arrivals, kept, given)
    input_grad = functools.reduce(jnp.add, [part.astype(jnp.float32) for part in parts])
    return tuple(out[None] for out in outs) + (input_grad.astype(jnp.bfloat16)[None],)


def solution(mesh):
    rows = P("exp", "ctx", None)
    experts = P("exp", None, None)
    return jax.shard_map(
        per_device,
        mesh=mesh,
        in_specs=(rows,) * 7 + (experts,) * 2,
        out_specs=(rows,) * 4,
        check_vma=False,
    )
```

time: 203 us -> 173 us (0.85)
  waiting for transfers between devices: 97.8 us -> 42.5 us
  Pallas kernels: 56.7 us -> 74.8 us
  blocking collectives: 14.4 us -> 0 us
  starting transfers between devices: 25.3 us -> 35.8 us
  other arithmetic: 3.01 us -> 10.3 us
  local copies, waits for them, and re-layouts: 4.83 us -> 7.58 us
    ppermute x15 -> x9, waiting for transfers between devices: 97.8 us -> 35.8 us  [move(): return lax.ppermute(block, 'exp', wide)]
    pallas_call x3 -> x4, Pallas kernels: 47.8 us -> 65.6 us  [expert_back(): pl.pallas_call(functools.partial(expert_kernel, sources, top), grid=(expe...]
    all_gather x1 -> x0, blocking collectives: 14.4 us -> none  [mixture_back(): metas = lax.all_gather(meta, 'exp')]
    all_to_all x0 -> x2, starting transfers between devices: none -> 7.88 us  [exchange(): lax.all_to_all(packed, 'ctx', split_axis=0, concat_axis=0, tiled=True)]
    all_to_all x0 -> x2, waiting for transfers between devices: none -> 3.74 us  [exchange(): lax.all_to_all(packed, 'ctx', split_axis=0, concat_axis=0, tiled=True)]
    unnamed x12 -> x34, local copies, waits for them, and re-layouts: 4.17 us -> 7.58 us
    convert_element_type x4 -> x3, other arithmetic: 1.02 us -> 4.37 us  [send_back(): both = move(both.astype(jnp.bfloat16), pairs)]
    ppermute x12 -> x9, waiting for transfers between devices: 0.03 us -> 2.98 us  [swap(): return lax.ppermute(block, 'exp', [(i, i ^ 1) for i in range(members)])]
  transfers between devices with their start and end apart: 27 -> 20, of which waited for: 9 -> 6; matrix products, arithmetic and copies ran while one was open for 1% -> 5% of each run, Pallas kernels for 28% -> 35%
where the time goes in v2:
time: 173 us; the launch traced here: 172 us
  Pallas kernels  74.8 us (43%)
  waiting for transfers between devices  42.5 us (25%)
  starting transfers between devices  35.8 us (21%)
  other arithmetic  10.3 us (6%)
  local copies, waits for them, and re-layouts  7.58 us (4%)
    pallas_call x4, Pallas kernels, expert_back(): pl.pallas_call(functools.partial(expert_kernel, sources, top), grid=(expe...  65.6 us
    ppermute x9, waiting for transfers between devices, move(): return lax.ppermute(block, 'exp', wide)  35.8 us
    ppermute x9, starting transfers between devices, move(): return lax.ppermute(block, 'exp', wide)  26.2 us
    all_to_all x2, starting transfers between devices, exchange(): lax.all_to_all(packed, 'ctx', split_axis=0, concat_axis=0, tiled=True)  7.88 us
    unnamed x34, local copies, waits for them, and re-layouts  7.58 us
    pallas_call x1, Pallas kernels, heads_back(): pl.pallas_call(heads_kernel, grid=(heads,), out_shape=jax.ShapeDtypeStruc...  6.24 us
    convert_element_type x3, other arithmetic, send_back(): both = move(both.astype(jnp.bfloat16), pairs)  4.37 us
    all_to_all x2, waiting for transfers between devices, exchange(): lax.all_to_all(packed, 'ctx', split_axis=0, concat_axis=0, tiled=True)  3.74 us
  transfers between devices with their start and end apart: 20, of which 6 were waited for; matrix products, arithmetic and copies ran while one was open for 5% of the time, Pallas kernels for 35%

profile of v2, /device:TPU:0, one launch (start us, length us, event | category | flops | bytes accessed | tf_op | source)
XLA Modules:
  0.0 171.9 jit_solution(13571992289791687011)
XLA Ops:
  0.6 0.8 copy.13
  1.4 0.8 copy.14
  2.2 1.0 copy-done
  3.3 1.0 copy-done.9
  4.3 0.2 make_block.1.refs_0_
  4.5 0.5 collective-permute-start.2
  5.0 1.3 collective-permute-start.1
  6.3 6.3 %collective-permute-start = (bf16[272,2048]{1,0:T(8,128)(2,1)S(1)}, bf16[272,2048]{1,0:T(8,128)(2,1)}, u32[]{:S(2)}, u32[]{:S(2)}) collective-permute-start(bf16[272,2048]{1,0:T(8,128)(2,1)S(1)} %make_block.1.refs_0_), channel_id=1, source_target_pairs={{0,2},{1,3},{2,4},{3,5},{4,6},{5,7},{8,10},{9,11},{10,12},{11,13},... | collective-permute-start | bytes 3342344 | tf_op jit(solution)/shard_map/ppermute | solution.py:263
  12.6 1.5 pack_groups.1
  14.1 4.2 %all-to-all-start = ((bf16[4,4,128,512]{3,2,1,0:T(8,128)(2,1)}), bf16[4,4,128,512]{3,2,1,0:T(8,128)(2,1)S(1)}, u32[]{:S(2)}, u32[]{:S(2)}) async-start(bf16[4,4,128,512]{3,2,1,0:T(8,128)(2,1)} %pack_groups.1), calls=%async_computation | async-start | bytes 4194304 | tf_op jit(solution)/shard_map/all_to_all | solution.py:118
  18.2 15.2 %expert_back.4 = (f32[128,2048]{1,0:T(8,128)S(1)}, bf16[128,2048]{1,0:T(8,128)(2,1)S(1)}) custom-call(s32[1]{0:T(128)} %bitcast.4.base_ref, bf16[272,2048]{1,0:T(8,128)(2,1)S(1)} %make_block.1.refs_0_, bf16[272,2048]{1,0:T(8,128)(2,1)} %collective-permute-done.2.refs_1_, bf16[4,2048,768]{2,1,0:T(8,128)(2,1)} %refs_2_.5, bf16[4,768,2048]{2,1,0:T(8,128)(2,1)} %refs_3_.5), custom_call_target="tpu_custom_call" | custom-call | flops 1811939328 | bytes 29360128 | tf_op jit(solution)/shard_map/expert_back/pallas_call | solution.py:218
  33.5 1.0 copy-done.3
  34.5 0.8 copy-done.13
  35.2 0.0 collective-permute-done.1.refs_2_
  35.3 0.6 collective-permute-done.refs_0_
  35.9 0.5 collective-permute-start.6
  36.4 1.6 collective-permute-start.3
  38.0 1.3 collective-permute-start.4
  39.3 3.7 %all-to-all-done.packed = bf16[4,4,128,512]{3,2,1,0:T(8,128)(2,1)S(1)} async-done(((bf16[4,4,128,512]{3,2,1,0:T(8,128)(2,1)}), bf16[4,4,128,512]{3,2,1,0:T(8,128)(2,1)S(1)}, u32[]{:S(2)}, u32[]{:S(2)}) %all-to-all-start) | async-done | bytes 2097184 | tf_op jit(solution)/shard_map/all_to_all | solution.py:118
  43.1 6.2 %heads_back.1 = bf16[4,3,128,512]{3,2,1,0:T(8,128)(2,1)S(1)} custom-call(bf16[4,4,128,512]{3,2,1,0:T(8,128)(2,1)S(1)} %all-to-all-done.packed), custom_call_target="tpu_custom_call" | custom-call | flops 2684354560 | bytes 3670016 | tf_op jit(solution)/shard_map/heads_back/pallas_call | solution.py:101
  49.3 1.1 copy-done.2
  50.5 0.0 collective-permute-done.5.refs_1_
  50.5 0.0 collective-permute-done.6.refs_3_
  50.5 19.1 %expert_back.5 = (f32[128,2048]{1,0:T(8,128)S(1)}, f32[128,2048]{1,0:T(8,128)S(1)}, bf16[256,2048]{1,0:T(8,128)(2,1)}) custom-call(s32[1]{0:T(128)} %bitcast.4.base_ref, bf16[272,2048]{1,0:T(8,128)(2,1)} %collective-permute-done.refs_0_, bf16[272,2048]{1,0:T(8,128)(2,1)S(1)} %collective-permute-done.5.refs_1_, ...), custom_call_target="tpu_custom_call" | custom-call | flops 3623878656 | bytes 33554432 | tf_op jit(solution)/shard_map/expert_back/pallas_call | solution.py:218
  69.6 0.0 collective-permute-start.11
  69.6 0.7 collective-permute-done.4
  70.3 1.4 broadcast_select_fusion.refs_0_
  71.7 0.1 collective-permute-start.8
  71.8 0.5 collective-permute-start.10
  72.3 1.3 collective-permute-start.7
  73.6 3.7 %all-to-all-start.1 = ((bf16[4,3,128,512]{3,2,1,0:T(8,128)(2,1)}), bf16[4,3,128,512]{3,2,1,0:T(8,128)(2,1)S(1)}, u32[]{:S(2)}, u32[]{:S(2)}) async-start(bf16[4,3,128,512]{3,2,1,0:T(8,128)(2,1)} %copy-done.2), calls=%async_computation.1 | async-start | bytes 3145728 | tf_op jit(solution)/shard_map/all_to_all | solution.py:118
  77.3 3.1 %add_convert_fusion.3 = (bf16[128,2048]{1,0:T(8,128)(2,1)}, bf16[128,2048]{1,0:T(8,128)(2,1)}) fusion(f32[128,2048]{1,0:T(8,128)} %copy-done.8, bf16[256,2048]{1,0:T(8,128)(2,1)} %collective-permute-done.11, f32[128,2048]{1,0:T(8,128)} %copy-done.7), kind=kLoop, calls=%fused_computation.4 | loop fusion | flops 1572864 | bytes 4194304 | tf_op jit(solution)/shard_map/convert_element_type | solution.py:285
  80.4 6.4 %collective-permute-start.13 = (bf16[128,2048]{1,0:T(8,128)(2,1)}, bf16[128,2048]{1,0:T(8,128)(2,1)}, u32[]{:S(2)}, u32[]{:S(2)}) collective-permute-start(bf16[128,2048]{1,0:T(8,128)(2,1)} %get-tuple-element.62), channel_id=1, source_target_pairs={{0,2},{1,3},{2,4},{3,5},{4,6},{5,7},{8,10},{9,11},{10,12},{11,13},... | collective-permute-start | bytes 1572872 | tf_op jit(solution)/shard_map/ppermute | solution.py:263
  86.8 1.6 collective-permute-start.12
  88.4 16.0 %expert_back.6 = (f32[128,2048]{1,0:T(8,128)S(1)}, bf16[128,2048]{1,0:T(8,128)(2,1)}) custom-call(s32[1]{0:T(128)} %bitcast.4.base_ref, bf16[272,2048]{1,0:T(8,128)(2,1)S(1)} %broadcast_select_fusion.refs_0_, bf16[272,2048]{1,0:T(8,128)(2,1)} %collective-permute-done.8.refs_1_, bf16[4,2048,768]{2,1,0:T(8,128)(2,1)} %refs_2_.5, bf16[4,768,2048]{2,1,0:T(8,128)(2,1)} %refs_3_.5), custom_call_target="tpu_custom_call" | custom-call | flops 1811939328 | bytes 29360128 | tf_op jit(solution)/shard_map/expert_back/pallas_call | solution.py:218
  104.4 1.0 copy-done.5
  105.4 2.1 %convert_add_fusion = f32[128,2048]{1,0:T(8,128)} fusion(f32[128,2048]{1,0:T(8,128)S(1)} %copy-done.4, bf16[128,2048]{1,0:T(8,128)(2,1)} %collective-permute-done.10), kind=kLoop, calls=%fused_computation.6 | loop fusion | flops 524288 | bytes 2621440 | tf_op jit(solution)/shard_map/add | solution.py:278
  107.6 1.2 unpack_groups.1
  108.8 3.5 %collective-permute-done.12 = bf16[128,2048]{1,0:T(8,128)(2,1)} collective-permute-done((bf16[128,2048]{1,0:T(8,128)(2,1)}, bf16[128,2048]{1,0:T(8,128)(2,1)}, u32[]{:S(2)}, u32[]{:S(2)}) %collective-permute-start.12) | collective-permute-done | bytes 524320 | tf_op jit(solution)/shard_map/ppermute | solution.py:263
  112.3 3.0 %collective-permute-done.15.refs_1_ = bf16[272,2048]{1,0:T(8,128)(2,1)S(1)} collective-permute-done((bf16[272,2048]{1,0:T(8,128)(2,1)}, bf16[272,2048]{1,0:T(8,128)(2,1)S(1)}, u32[]{:S(2)}, u32[]{:S(2)}) %collective-permute-start.15) | collective-permute-done | bytes 1114144 | tf_op jit(solution)/shard_map/ppermute | solution.py:259
  115.2 15.2 %expert_back.7 = (f32[128,2048]{1,0:T(8,128)S(1)}, bf16[128,2048]{1,0:T(8,128)(2,1)S(1)}) custom-call(s32[1]{0:T(128)} %bitcast.4.base_ref, bf16[272,2048]{1,0:T(8,128)(2,1)} %collective-permute-done.7.refs_0_, bf16[272,2048]{1,0:T(8,128)(2,1)S(1)} %collective-permute-done.15.refs_1_, bf16[4,2048,768]{2,1,0:T(8,128)(2,1)} %refs_2_.5, ...), custom_call_target="tpu_custom_call" | custom-call | flops 1811939328 | bytes 29360128 | tf_op jit(solution)/shard_map/expert_back/pallas_call | solution.py:218
  130.5 0.2 collective-permute-start.16
  130.7 1.1 add_convert_fusion.2
  131.8 2.1 %collective-permute-start.14 = (bf16[128,2048]{1,0:T(8,128)(2,1)S(1)}, bf16[128,2048]{1,0:T(8,128)(2,1)S(1)}, u32[]{:S(2)}, u32[]{:S(2)}) collective-permute-start(bf16[128,2048]{1,0:T(8,128)(2,1)S(1)} %add_convert_fusion.2), channel_id=1, source_target_pairs={{4,0},{5,1},{6,2},{7,3},{0,4},{1,5},{2,6},{3,7},{12,8},{13,9},{14,... | collective-permute-start | bytes 1572872 | tf_op jit(solution)/shard_map/ppermute | solution.py:263
  133.9 0.1 add_convert_fusion.1
  134.1 4.4 %collective-permute-start.17 = (bf16[128,2048]{1,0:T(8,128)(2,1)S(1)}, bf16[128,2048]{1,0:T(8,128)(2,1)S(1)}, u32[]{:S(2)}, u32[]{:S(2)}) collective-permute-start(bf16[128,2048]{1,0:T(8,128)(2,1)S(1)} %add_convert_fusion.1), channel_id=1, source_target_pairs={{6,0},{7,1},{0,6},{1,7},{14,8},{15,9},{8,14},{9,15},{22,16},{23,17... | collective-permute-start | bytes 1572872 | tf_op jit(solution)/shard_map/ppermute | solution.py:263
  138.4 31.1 %collective-permute-done.14 = bf16[128,2048]{1,0:T(8,128)(2,1)S(1)} collective-permute-done((bf16[128,2048]{1,0:T(8,128)(2,1)S(1)}, bf16[128,2048]{1,0:T(8,128)(2,1)S(1)}, u32[]{:S(2)}, u32[]{:S(2)}) %collective-permute-start.14) | collective-permute-done | bytes 524320 | tf_op jit(solution)/shard_map/ppermute | solution.py:263
  169.5 2.4 %fusion = bf16[1,128,2048]{2,1,0:T(8,128)(2,1)} fusion(bf16[128,2048]{1,0:T(8,128)(2,1)S(1)} %collective-permute-done.17, bf16[128,2048]{1,0:T(8,128)(2,1)S(1)} %collective-permute-done.14, bf16[128,2048]{1,0:T(8,128)(2,1)} %collective-permute-done.13, f32[128,2048]{1,0:T(8,128)S(1)} %copy-done.15, bf16[128,2048]{1,0:T(8,128)(2,1)} %collective-permute-done.12), kind=kLoop, calls=%fused_computation.7 | loop fusion | flops 2359296 | bytes 3670016 | tf_op jit(solution)/shard_map/broadcast_in_dim | solution.py:317
  (40 shorter events, 0.1 us)
Async XLA Ops:
  2.2 1.0 copy-start
  3.2 1.0 copy-start.9
  4.3 8.3 %copy-start.1 = (bf16[1,128,2048]{2,1,0:T(8,128)(2,1)S(1)}, bf16[1,128,2048]{2,1,0:T(8,128)(2,1)}, u32[]{:S(2)}) copy-start(bf16[1,128,2048]{2,1,0:T(8,128)(2,1)} %param.12) | copy-start | bytes 1572868
  4.3 8.3 %copy-start.10 = (bf16[1,128,2048]{2,1,0:T(8,128)(2,1)S(1)}, bf16[1,128,2048]{2,1,0:T(8,128)(2,1)}, u32[]{:S(2)}) copy-start(bf16[1,128,2048]{2,1,0:T(8,128)(2,1)} %param.9) | copy-start | bytes 1572868
  4.3 8.3 %copy-start.11 = (bf16[1,128,2048]{2,1,0:T(8,128)(2,1)S(1)}, bf16[1,128,2048]{2,1,0:T(8,128)(2,1)}, u32[]{:S(2)}) copy-start(bf16[1,128,2048]{2,1,0:T(8,128)(2,1)} %param.10) | copy-start | bytes 1572868
  4.3 8.3 %copy-start.12 = (bf16[1,128,2048]{2,1,0:T(8,128)(2,1)S(1)}, bf16[1,128,2048]{2,1,0:T(8,128)(2,1)}, u32[]{:S(2)}) copy-start(bf16[1,128,2048]{2,1,0:T(8,128)(2,1)} %param.11) | copy-start | bytes 1572868
  4.5 13.7 %collective-permute-start.2 = (bf16[272,2048]{1,0:T(8,128)(2,1)S(1)}, bf16[272,2048]{1,0:T(8,128)(2,1)}, u32[]{:S(2)}, u32[]{:S(2)}) collective-permute-start(bf16[272,2048]{1,0:T(8,128)(2,1)S(1)} %make_block.1.refs_0_), channel_id=1, source_target_pairs={{0,1},{1,0},{2,3},{3,2},{4,5},{5,4},{6,7},{7,6},{8,9},{9,8},{10,11... | collective-permute-start | bytes 3342344 | tf_op jit(solution)/shard_map/ppermute | solution.py:259
  5.0 30.3 %collective-permute-start.1 = (bf16[272,2048]{1,0:T(8,128)(2,1)S(1)}, bf16[272,2048]{1,0:T(8,128)(2,1)}, u32[]{:S(2)}, u32[]{:S(2)}) collective-permute-start(bf16[272,2048]{1,0:T(8,128)(2,1)S(1)} %make_block.1.refs_0_), channel_id=1, source_target_pairs={{2,0},{3,1},{4,2},{5,3},{6,4},{7,5},{10,8},{11,9},{12,10},{13,11},... | collective-permute-start | bytes 3342344 | tf_op jit(solution)/shard_map/ppermute | solution.py:263
  6.3 29.6 %collective-permute-start = (bf16[272,2048]{1,0:T(8,128)(2,1)S(1)}, bf16[272,2048]{1,0:T(8,128)(2,1)}, u32[]{:S(2)}, u32[]{:S(2)}) collective-permute-start(bf16[272,2048]{1,0:T(8,128)(2,1)S(1)} %make_block.1.refs_0_), channel_id=1, source_target_pairs={{0,2},{1,3},{2,4},{3,5},{4,6},{5,7},{8,10},{9,11},{10,12},{11,13},... | collective-permute-start | bytes 3342344 | tf_op jit(solution)/shard_map/ppermute | solution.py:263
  14.1 29.0 %all-to-all-start = ((bf16[4,4,128,512]{3,2,1,0:T(8,128)(2,1)}), bf16[4,4,128,512]{3,2,1,0:T(8,128)(2,1)S(1)}, u32[]{:S(2)}, u32[]{:S(2)}) async-start(bf16[4,4,128,512]{3,2,1,0:T(8,128)(2,1)} %pack_groups.1), calls=%async_computation | async-start | bytes 4194304 | tf_op jit(solution)/shard_map/all_to_all | solution.py:118
  33.5 1.0 copy-start.3
  34.5 0.8 copy-start.13
  35.9 14.6 %collective-permute-start.5 = (bf16[272,2048]{1,0:T(8,128)(2,1)}, bf16[272,2048]{1,0:T(8,128)(2,1)S(1)}, u32[]{:S(2)}, u32[]{:S(2)}) collective-permute-start(bf16[272,2048]{1,0:T(8,128)(2,1)} %collective-permute-done.refs_0_), channel_id=1, source_target_pairs={{0,1},{1,0},{2,3},{3,2},{4,5},{5,4},{6,7},{7,6},{8,9},{9,8},{10,11... | collective-permute-start | bytes 3342344 | tf_op jit(solution)/shard_map/ppermute | solution.py:259
  35.9 14.6 %collective-permute-start.6 = (bf16[272,2048]{1,0:T(8,128)(2,1)}, bf16[272,2048]{1,0:T(8,128)(2,1)}, u32[]{:S(2)}, u32[]{:S(2)}) collective-permute-start(bf16[272,2048]{1,0:T(8,128)(2,1)} %collective-permute-done.1.refs_2_), channel_id=1, source_target_pairs={{0,1},{1,0},{2,3},{3,2},{4,5},{5,4},{6,7},{7,6},{8,9},{9,8},{10,11... | collective-permute-start | bytes 3342344 | tf_op jit(solution)/shard_map/ppermute | solution.py:259
  36.4 33.2 %collective-permute-start.3 = (bf16[272,2048]{1,0:T(8,128)(2,1)}, bf16[272,2048]{1,0:T(8,128)(2,1)}, u32[]{:S(2)}, u32[]{:S(2)}) collective-permute-start(bf16[272,2048]{1,0:T(8,128)(2,1)} %collective-permute-done.refs_0_), channel_id=1, source_target_pairs={{2,4},{3,5},{4,6},{5,7},{10,12},{11,13},{12,14},{13,15},{18,20},{1... | collective-permute-start | bytes 3342344 | tf_op jit(solution)/shard_map/ppermute | solution.py:263
  38.0 32.2 %collective-permute-start.4 = (bf16[272,2048]{1,0:T(8,128)(2,1)}, bf16[272,2048]{1,0:T(8,128)(2,1)}, u32[]{:S(2)}, u32[]{:S(2)}) collective-permute-start(bf16[272,2048]{1,0:T(8,128)(2,1)} %collective-permute-done.1.refs_2_), channel_id=1, source_target_pairs={{2,0},{3,1},{4,2},{5,3},{10,8},{11,9},{12,10},{13,11},{18,16},{19,... | collective-permute-start | bytes 3342344 | tf_op jit(solution)/shard_map/ppermute | solution.py:263
  49.3 1.2 copy-start.2
  69.6 2.1 %copy-start.7 = (f32[128,2048]{1,0:T(8,128)}, f32[128,2048]{1,0:T(8,128)S(1)}, u32[]{:S(2)}) copy-start(f32[128,2048]{1,0:T(8,128)S(1)} %get-tuple-element.44) | copy-start | bytes 3145732
  69.6 2.1 %copy-start.8 = (f32[128,2048]{1,0:T(8,128)}, f32[128,2048]{1,0:T(8,128)S(1)}, u32[]{:S(2)}) copy-start(f32[128,2048]{1,0:T(8,128)S(1)} %get-tuple-element.46) | copy-start | bytes 3145732
  69.6 7.7 %collective-permute-start.11 = (bf16[256,2048]{1,0:T(8,128)(2,1)}, bf16[256,2048]{1,0:T(8,128)(2,1)}, u32[]{:S(2)}, u32[]{:S(2)}) collective-permute-start(bf16[256,2048]{1,0:T(8,128)(2,1)} %get-tuple-element.45), channel_id=1, source_target_pairs={{0,1},{1,0},{2,3},{3,2},{4,5},{5,4},{6,7},{7,6},{8,9},{9,8},{10,11... | collective-permute-start | bytes 3145736 | tf_op jit(solution)/shard_map/ppermute | solution.py:259
  70.3 1.5 copy-start.14
  71.7 16.7 %collective-permute-start.8 = (bf16[272,2048]{1,0:T(8,128)(2,1)S(1)}, bf16[272,2048]{1,0:T(8,128)(2,1)}, u32[]{:S(2)}, u32[]{:S(2)}) collective-permute-start(bf16[272,2048]{1,0:T(8,128)(2,1)S(1)} %broadcast_select_fusion.refs_0_), channel_id=1, source_target_pairs={{0,1},{1,0},{2,3},{3,2},{4,5},{5,4},{6,7},{7,6},{8,9},{9,8},{10,11... | collective-permute-start | bytes 3342344 | tf_op jit(solution)/shard_map/ppermute | solution.py:259
  71.8 33.6 %collective-permute-start.10 = (bf16[128,2048]{1,0:T(8,128)(2,1)S(1)}, bf16[128,2048]{1,0:T(8,128)(2,1)}, u32[]{:S(2)}, u32[]{:S(2)}) collective-permute-start(bf16[128,2048]{1,0:T(8,128)(2,1)S(1)} %copy-done.14), channel_id=1, source_target_pairs={{0,1},{1,0},{2,3},{3,2},{4,5},{5,4},{6,7},{7,6},{8,9},{9,8},{10,11... | collective-permute-start | bytes 1572872 | tf_op jit(solution)/shard_map/ppermute | solution.py:259
  72.3 36.5 %collective-permute-start.7 = (bf16[272,2048]{1,0:T(8,128)(2,1)S(1)}, bf16[272,2048]{1,0:T(8,128)(2,1)}, u32[]{:S(2)}, u32[]{:S(2)}) collective-permute-start(bf16[272,2048]{1,0:T(8,128)(2,1)S(1)} %broadcast_select_fusion.refs_0_), channel_id=1, source_target_pairs={{4,6},{5,7},{2,0},{3,1},{12,14},{13,15},{10,8},{11,9},{20,22},{21,... | collective-permute-start | bytes 3342344 | tf_op jit(solution)/shard_map/ppermute | solution.py:263
  73.6 34.0 %all-to-all-start.1 = ((bf16[4,3,128,512]{3,2,1,0:T(8,128)(2,1)}), bf16[4,3,128,512]{3,2,1,0:T(8,128)(2,1)S(1)}, u32[]{:S(2)}, u32[]{:S(2)}) async-start(bf16[4,3,128,512]{3,2,1,0:T(8,128)(2,1)} %copy-done.2), calls=%async_computation.1 | async-start | bytes 3145728 | tf_op jit(solution)/shard_map/all_to_all | solution.py:118
  80.4 28.4 %collective-permute-start.13 = (bf16[128,2048]{1,0:T(8,128)(2,1)}, bf16[128,2048]{1,0:T(8,128)(2,1)}, u32[]{:S(2)}, u32[]{:S(2)}) collective-permute-start(bf16[128,2048]{1,0:T(8,128)(2,1)} %get-tuple-element.62), channel_id=1, source_target_pairs={{0,2},{1,3},{2,4},{3,5},{4,6},{5,7},{8,10},{9,11},{10,12},{11,13},... | collective-permute-start | bytes 1572872 | tf_op jit(solution)/shard_map/ppermute | solution.py:263
  86.8 18.6 %copy-start.4 = (f32[128,2048]{1,0:T(8,128)S(1)}, f32[128,2048]{1,0:T(8,128)}, u32[]{:S(2)}) copy-start(f32[128,2048]{1,0:T(8,128)} %copy-done.3) | copy-start | bytes 3145732
  86.8 25.5 %collective-permute-start.12 = (bf16[128,2048]{1,0:T(8,128)(2,1)}, bf16[128,2048]{1,0:T(8,128)(2,1)}, u32[]{:S(2)}, u32[]{:S(2)}) collective-permute-start(bf16[128,2048]{1,0:T(8,128)(2,1)} %get-tuple-element.63), channel_id=1, source_target_pairs={{2,0},{3,1},{4,2},{5,3},{6,4},{7,5},{10,8},{11,9},{12,10},{13,11},... | collective-permute-start | bytes 1572872 | tf_op jit(solution)/shard_map/ppermute | solution.py:263
  104.4 1.0 copy-start.5
  105.4 6.9 %collective-permute-start.9 = (bf16[128,2048]{1,0:T(8,128)(2,1)}, bf16[128,2048]{1,0:T(8,128)(2,1)}, u32[]{:S(2)}, u32[]{:S(2)}) collective-permute-start(bf16[128,2048]{1,0:T(8,128)(2,1)} %get-tuple-element.41), channel_id=1, source_target_pairs={{0,1},{1,0},{2,3},{3,2},{4,5},{5,4},{6,7},{7,6},{8,9},{9,8},{10,11... | collective-permute-start | bytes 1572872 | tf_op jit(solution)/shard_map/ppermute | solution.py:259
  112.3 18.4 %copy-start.6 = (f32[128,2048]{1,0:T(8,128)S(1)}, f32[128,2048]{1,0:T(8,128)}, u32[]{:S(2)}) copy-start(f32[128,2048]{1,0:T(8,128)} %copy-done.5) | copy-start | bytes 3145732
  112.3 3.0 %collective-permute-start.15 = (bf16[272,2048]{1,0:T(8,128)(2,1)}, bf16[272,2048]{1,0:T(8,128)(2,1)S(1)}, u32[]{:S(2)}, u32[]{:S(2)}) collective-permute-start(bf16[272,2048]{1,0:T(8,128)(2,1)} %collective-permute-done.7.refs_0_), channel_id=1, source_target_pairs={{0,1},{1,0},{2,3},{3,2},{4,5},{5,4},{6,7},{7,6},{8,9},{9,8},{10,11... | collective-permute-start | bytes 3342344 | tf_op jit(solution)/shard_map/ppermute | solution.py:259
  130.5 3.5 %collective-permute-start.16 = (bf16[128,2048]{1,0:T(8,128)(2,1)S(1)}, bf16[128,2048]{1,0:T(8,128)(2,1)S(1)}, u32[]{:S(2)}, u32[]{:S(2)}) collective-permute-start(bf16[128,2048]{1,0:T(8,128)(2,1)S(1)} %get-tuple-element.61), channel_id=1, source_target_pairs={{0,1},{1,0},{2,3},{3,2},{4,5},{5,4},{6,7},{7,6},{8,9},{9,8},{10,11... | collective-permute-start | bytes 1572872 | tf_op jit(solution)/shard_map/ppermute | solution.py:259
  131.8 37.7 %copy-start.15 = (f32[128,2048]{1,0:T(8,128)S(1)}, f32[128,2048]{1,0:T(8,128)}, u32[]{:S(2)}) copy-start(f32[128,2048]{1,0:T(8,128)} %convert_add_fusion) | copy-start | bytes 3145732
  131.8 37.6 %collective-permute-start.14 = (bf16[128,2048]{1,0:T(8,128)(2,1)S(1)}, bf16[128,2048]{1,0:T(8,128)(2,1)S(1)}, u32[]{:S(2)}, u32[]{:S(2)}) collective-permute-start(bf16[128,2048]{1,0:T(8,128)(2,1)S(1)} %add_convert_fusion.2), channel_id=1, source_target_pairs={{4,0},{5,1},{6,2},{7,3},{0,4},{1,5},{2,6},{3,7},{12,8},{13,9},{14,... | collective-permute-start | bytes 1572872 | tf_op jit(solution)/shard_map/ppermute | solution.py:263
  134.1 35.4 %collective-permute-start.17 = (bf16[128,2048]{1,0:T(8,128)(2,1)S(1)}, bf16[128,2048]{1,0:T(8,128)(2,1)S(1)}, u32[]{:S(2)}, u32[]{:S(2)}) collective-permute-start(bf16[128,2048]{1,0:T(8,128)(2,1)S(1)} %add_convert_fusion.1), channel_id=1, source_target_pairs={{6,0},{7,1},{0,6},{1,7},{14,8},{15,9},{8,14},{9,15},{22,16},{23,17... | collective-permute-start | bytes 1572872 | tf_op jit(solution)/shard_map/ppermute | solution.py:263
